TPU v7x, 128 devices: a whole 4x4x4 slice. The times are simulated.
128 devices in a mesh: sec: 2 (over core), req: 16 (over z, y), kv: 4 (over x).
Axes of the slice: x: 4, y: 4, z: 4, core: 2. Of those that a mesh axis runs over, the one named last changes fastest.
Arguments:
- queries: bfloat16 [2048, 4096], P('req', ('kv', 'sec')), may hold values from -21 to 21
- key_cache: bfloat16 [2048, 4, 32, 128], P('req', 'kv'), may hold values from -21 to 21
- value_cache: bfloat16 [2048, 4, 32, 128], P('req', 'kv'), may hold values from -18 to 18
- new_keys: bfloat16 [2048, 4, 128], P('req', 'kv'), may hold values from -5 to 5
- new_values: bfloat16 [2048, 4, 128], P('req', 'kv'), may hold values from -18 to 18
- lengths: int32 [2048], P('req'), may hold values from 2 to 32
- out_proj: bfloat16 [4096, 4096], P(('kv', 'sec')), may hold values from -0.09375 to 0.09375
- residual: bfloat16 [2048, 4096], P(('req', 'sec', 'kv')), may hold values from -36 to 36
- norm_gain: float32 [4096], replicated, may hold values from 0.1 to 1.9
- expert_ids: int32 [2048, 8], P(('req', 'sec', 'kv')), may hold values from 0 to 127, as said below
- expert_slots: int32 [2048, 8], P(('req', 'sec', 'kv')), may hold values from 0 to 1, as said below
- gate_probs: float32 [2048, 8], P(('req', 'sec', 'kv')), may hold values from 0.1 to 0.4
- w_gate: bfloat16 [128, 4096, 768], P(('sec', 'req', 'kv')), may hold values from -0.09375 to 0.09375
- w_up: bfloat16 [128, 4096, 768], P(('sec', 'req', 'kv')), may hold values from -0.09375 to 0.09375
- w_down: bfloat16 [128, 768, 4096], P(('sec', 'req', 'kv')), may hold values from -0.21875 to 0.21875
Outputs:
- stream: bfloat16 [2048, 4096], P(('req', 'sec', 'kv'))
- moe_out: bfloat16 [2048, 4096], P(('req', 'sec', 'kv'))
Inputs may be any that keep to these rules, and one draw needn't show every extreme that they name: `expert_ids`: each row names 8 different experts. In each block of 16 consecutive rows (the rows of one device) every expert is named at least 0 and at most 2 times, and one expert, the same for all blocks, exactly 2 times. `expert_slots`: within a block the entries naming one expert hold different slots, numbered from 0 in row order.
All inputs are finite; a program needn't handle non-finite values.
Results may differ from a plain program's by a relative error of at most 0.029.
Values may be sent and summed in bfloat16 or wider, within the bound.
No kernel may reach another device: no remote copies, remote signals or barrier semaphores. Data moves between devices by JAX's collectives and lax.ppermute only.
A program may use at most 128 MiB of HBM per device.

v0:
```python
import jax
import jax.numpy as jnp
from jax import lax
from jax.sharding import PartitionSpec as P


def on_device(
    queries,
    key_cache,
    value_cache,
    new_keys,
    new_values,
    lengths,
    out_proj,
    residual,
    norm_gain,
    expert_ids,
    expert_slots,
    gate_probs,
    w_gate,
    w_up,
    w_down,
):
    row_count, head_width = queries.shape
    head_size = key_cache.shape[3]
    positions = key_cache.shape[2]
    heads_here = head_width // head_size
    width = out_proj.shape[1]
    score_scale = 1.0 / head_size**0.5
    query_heads = queries.reshape(row_count, heads_here, head_size)
    score = (
        jnp.einsum("thd,tpd->thp", query_heads, key_cache[:, 0], preferred_element_type=jnp.float32)
        * score_scale
    )
    own_score = (
        jnp.einsum("thd,td->th", query_heads, new_keys[:, 0], preferred_element_type=jnp.float32)
        * score_scale
    )
    valid = jnp.arange(positions, dtype=jnp.int32)[None, :] < lengths[:, None]
    score = jnp.where(valid[:, None, :], score, -jnp.inf)
    highest = jnp.maximum(jnp.max(score, axis=-1), own_score)
    raised = jnp.exp(score - highest[..., None])
    own_raised = jnp.exp(own_score - highest)
    denominator = jnp.sum(raised, axis=-1) + own_raised
    weight = (raised / denominator[..., None]).astype(jnp.bfloat16)
    own_weight = (own_raised / denominator).astype(jnp.bfloat16)
    attn = jnp.einsum("thp,tpd->thd", weight, value_cache[:, 0], preferred_element_type=jnp.float32)
    attn = (
        attn
        + own_weight.astype(jnp.float32)[..., None]
        * new_values[:, 0].astype(jnp.float32)[:, None, :]
    )
    attn = attn.astype(jnp.bfloat16).reshape(row_count, head_width)
    sec_count = lax.axis_size("sec")
    group_count = lax.axis_size("kv")
    row_share = row_count // (sec_count * group_count)
    proj = lax.psum_scatter(
        jnp.dot(attn, out_proj, preferred_element_type=jnp.float32).astype(jnp.bfloat16),
        ("sec", "kv"),
        scatter_dimension=0,
        tiled=True,
    ).astype(jnp.float32)
    stream = (residual.astype(jnp.float32) + proj).astype(jnp.bfloat16)
    widened = lax.optimization_barrier(stream).astype(jnp.float32)
    mean_square = jnp.mean(widened * widened, axis=-1, keepdims=True)
    normed = (widened * lax.rsqrt(mean_square + 1e-06) * norm_gain).astype(jnp.bfloat16)
    expert_count = sec_count * lax.axis_size("req") * group_count
    top_count = expert_ids.shape[1]
    capacity = top_count * row_share // expert_count + 1
    slot_index = (expert_ids * capacity + expert_slots).reshape(-1)
    repeated = jnp.broadcast_to(normed[:, None, :], (row_share, top_count, width)).reshape(
        row_share * top_count, width
    )
    outgoing = (
        jnp.zeros((expert_count * capacity, width), jnp.bfloat16).at[slot_index].set(repeated)
    )
    arrived = lax.all_to_all(
        outgoing.reshape(expert_count, capacity, width),
        ("sec", "req", "kv"),
        split_axis=0,
        concat_axis=0,
        tiled=True,
    )
    flat_rows = arrived.reshape(-1, width)
    gate_out = jnp.dot(flat_rows, w_gate[0], preferred_element_type=jnp.float32)
    up_out = jnp.dot(flat_rows, w_up[0], preferred_element_type=jnp.float32)
    hidden = (jax.nn.silu(gate_out) * up_out).astype(jnp.bfloat16)
    finished = jnp.dot(hidden, w_down[0], preferred_element_type=jnp.float32).astype(jnp.bfloat16)
    returned = lax.all_to_all(
        finished.reshape(arrived.shape),
        ("sec", "req", "kv"),
        split_axis=0,
        concat_axis=0,
        tiled=True,
    )
    picked = returned.reshape(expert_count * capacity, width)[slot_index].reshape(
        row_share, top_count, width
    )
    moe_out = jnp.sum(picked.astype(jnp.float32) * gate_probs[..., None], axis=1).astype(
        jnp.bfloat16
    )
    return (stream, moe_out)


def solution(mesh):
    return jax.shard_map(
        on_device,
        mesh=mesh,
        in_specs=(
            P("req", ("kv", "sec")),
            P("req", "kv", None, None),
            P("req", "kv", None, None),
            P("req", "kv", None),
            P("req", "kv", None),
            P("req"),
            P(("kv", "sec"), None),
            P(("req", "sec", "kv"), None),
            P(),
            P(("req", "sec", "kv"), None),
            P(("req", "sec", "kv"), None),
            P(("req", "sec", "kv"), None),
            P(("sec", "req", "kv"), None, None),
            P(("sec", "req", "kv"), None, None),
            P(("sec", "req", "kv"), None, None),
        ),
        out_specs=(P(("req", "sec", "kv"), None), P(("req", "sec", "kv"), None)),
        check_vma=False,
    )
```

profile of v0, /device:TPU:1, one launch (start us, length us, event | category | flops | bytes accessed | tf_op | source)
XLA Modules:
  0.0 170.9 jit_solution(12897851394321069817)
XLA Ops:
  7.2 0.0 copy-start
  7.2 0.0 copy-start.4
  7.2 0.0 reduce-scatter.2.cloned.1.call-start
  7.2 1.0 reshape.90
  8.3 0.7 iota_compare_fusion
  9.0 2.0 %fusion.42 = (f32[128,4]{1,0:T(8,128)S(1)}, f32[128,4,32]{2,1,0:T(4,128)S(1)}) fusion(bf16[128,4,128]{2,1,0:T(4,128)(2,1)S(1)} %reshape.90, bf16[128,1,32,128]{3,2,1,0:T(8,128)(2,1)} %param.16, pred[128,32]{1,0:T(8,128)(4,1)S(1)} %iota_compare_fusion), kind=kOutput, calls=%fused_computation.54 | convolution fusion | flops 4242944 | bytes 1251328 | tf_op jit(solution)/shard_map/thd,tpd->thp/dot_general | solution.py:32
  11.0 0.1 copy.26
  11.0 1.1 fusion.35
  12.1 0.1 copy.34
  12.1 0.1 copy.27
  12.3 0.4 fusion.30
  12.7 0.1 copy.28
  12.8 0.1 copy.29
  12.9 0.1 copy.30
  13.0 0.0 copy-done.4
  13.0 0.0 copy-done
  13.0 0.5 fusion.17
  13.5 0.0 copy-start.6
  13.5 0.0 copy-start.7
  13.5 0.0 copy-start.3
  13.6 0.0 copy-start.5
  13.6 3.9 %convolution_convert_fusion = bf16[128,4096]{1,0:T(8,128)(2,1)} fusion(bf16[512,4096]{1,0:T(8,128)(2,1)} %param.21, bf16[16,8,4,128]{3,2,1,0:T(4,128)(2,1)S(1)} %bitcast.63), kind=kOutput, calls=%fused_computation.9 | convolution fusion | flops 537395200 | bytes 5373952 | tf_op jit(solution)/shard_map/dot_general | solution.py:58
  17.5 0.0 reduce-scatter.2.cloned.1.call-update
  17.5 0.0 copy-done.6
  17.5 0.0 copy-done.7
  17.6 0.1 copy.31
  17.6 0.1 reshape.92
  17.7 37.4 %reduce-scatter.2.cloned.1.call-done = bf16[16,4096]{1,0:T(8,128)(2,1)} async-done(((bf16[128,4096]{1,0:T(8,128)(2,1)}), bf16[16,4096]{1,0:T(8,128)(2,1)}) %reduce-scatter.2.cloned.1.call-update) | async-done | bytes 131088 | tf_op jit(solution)/shard_map/reduce_scatter | solution.py:57
  55.2 0.0 copy-done.3
  55.2 0.9 add_convert_fusion
  56.1 0.0 copy-start.2
  56.1 0.1 fusion.27
  56.3 0.0 copy-done.5
  56.3 0.1 fusion.29
  56.4 2.7 %scatter_custom_fusion = bf16[256,4096]{1,0:T(8,128)(2,1)S(1)} fusion(s32[128]{0:T(128)S(1)} %fusion.39, bf16[]{:T(256)} %constant.4.clone.1, bf16[16,4096]{1,0:T(8,128)(2,1)S(1)} %fusion.29), kind=kCustom, calls=%fused_computation.18 | custom fusion | bytes 2228226 | tf_op jit(solution)/shard_map/scatter | solution.py:75
  59.1 2.7 %reshape.94 = bf16[128,2,4096]{2,1,0:T(2,128)(2,1)} reshape(bf16[256,4096]{1,0:T(8,128)(2,1)S(1)} %scatter_custom_fusion) | data formatting | bytes 4194304 | tf_op jit(solution)/shard_map/reshape | solution.py:78
  61.8 0.0 copy-done.2
  61.8 36.2 %all_to_all.10 = bf16[128,2,4096]{2,1,0:T(2,128)(2,1)S(1)} all-to-all(bf16[128,2,4096]{2,1,0:T(2,128)(2,1)} %reshape.94), channel_id=1, replica_groups=mesh['sec'=2,'req'=16,'kv'=4] {'sec','req','kv'}, dimensions={0} | all-to-all | bytes 4194304 | tf_op jit(solution)/shard_map/all_to_all | solution.py:77
  98.0 2.2 %reshape.95 = bf16[256,4096]{1,0:T(8,128)(2,1)} reshape(bf16[128,2,4096]{2,1,0:T(2,128)(2,1)S(1)} %all_to_all.10) | data formatting | bytes 4194304 | tf_op jit(solution)/shard_map/reshape | solution.py:84
  100.2 0.0 copy-start.1
  100.2 6.3 %fusion.4 = f32[256,768]{1,0:T(8,128)} fusion(bf16[256,4096]{1,0:T(8,128)(2,1)} %reshape.95, bf16[1,4096,768]{2,1,0:T(8,128)(2,1)} %param.27), kind=kOutput, calls=%fused_computation.6 | convolution fusion | flops 1610612736 | bytes 9175040 | tf_op jit(solution)/shard_map/dot_general | solution.py:85
  106.5 0.0 copy-done.1
  106.5 10.7 %fusion.6 = bf16[256,4096]{1,0:T(8,128)(2,1)} fusion(bf16[1,768,4096]{2,1,0:T(8,128)(2,1)} %param.29, bf16[256,4096]{1,0:T(8,128)(2,1)S(1)} %copy-done.1, bf16[1,4096,768]{2,1,0:T(8,128)(2,1)} %param.28, f32[256,768]{1,0:T(8,128)} %fusion.4), kind=kOutput, calls=%fused_computation.8 | convolution fusion | flops 3223453696 | bytes 17563648 | tf_op jit(solution)/shard_map/dot_general | solution.py:88
  117.2 4.4 %reshape.96 = bf16[128,2,4096]{2,1,0:T(2,128)(2,1)} reshape(bf16[256,4096]{1,0:T(8,128)(2,1)} %fusion.6) | data formatting | bytes 4194304 | tf_op jit(solution)/shard_map/reshape | solution.py:90
  121.6 0.0 copy-start.8
  121.6 6.5 %all-to-all-start.1 = ((bf16[128,2,4096]{2,1,0:T(2,128)(2,1)}), bf16[128,2,4096]{2,1,0:T(2,128)(2,1)}, u32[]{:S(2)}, u32[]{:S(2)}) async-start(bf16[128,2,4096]{2,1,0:T(2,128)(2,1)} %reshape.96), calls=%async_computation.2 | async-start | bytes 4194304 | tf_op jit(solution)/shard_map/all_to_all | solution.py:89
  128.1 0.0 copy-done.8
  128.2 0.1 copy.32
  128.2 28.2 %all-to-all-done.1 = bf16[128,2,4096]{2,1,0:T(2,128)(2,1)} async-done(((bf16[128,2,4096]{2,1,0:T(2,128)(2,1)}), bf16[128,2,4096]{2,1,0:T(2,128)(2,1)}, u32[]{:S(2)}, u32[]{:S(2)}) %all-to-all-start.1) | async-done | bytes 2097184 | tf_op jit(solution)/shard_map/all_to_all | solution.py:89
  156.4 2.7 %reshape.97 = bf16[256,4096]{1,0:T(8,128)(2,1)S(1)} reshape(bf16[128,2,4096]{2,1,0:T(2,128)(2,1)} %all-to-all-done.1) | data formatting | bytes 4194304 | tf_op jit(solution)/shard_map/reshape | solution.py:96
  159.1 2.2 %gather_fusion = bf16[128,4096]{1,0:T(8,128)(2,1)} fusion(bf16[256,4096]{1,0:T(8,128)(2,1)S(1)} %reshape.97, s32[1024]{0:T(1024)S(1)} %pad_clamp_fusion), kind=kCustom, calls=%fused_computation | custom fusion | bytes 2097664 | tf_op jit(solution)/shard_map/gather | solution.py:96
  161.3 2.7 %fusion.9 = bf16[16,4096]{1,0:T(8,128)(2,1)} fusion(bf16[128,4096]{1,0:T(8,128)(2,1)} %gather_fusion, f32[16,8]{1,0:T(8,128)S(1)} %copy.32), kind=kLoop, calls=%fused_computation.11 | loop fusion | flops 1507328 | bytes 1180160 | tf_op jit(solution)/shard_map/reduce_sum | solution.py:99
  (7 shorter events, 0.1 us)
Async XLA Ops:
  7.2 5.9 %copy-start = (bf16[128,1,32,128]{3,2,1,0:T(8,128)(2,1)S(1)}, bf16[128,1,32,128]{3,2,1,0:T(8,128)(2,1)}, u32[]{:S(2)}) copy-start(bf16[128,1,32,128]{3,2,1,0:T(8,128)(2,1)} %param.17) | copy-start | bytes 3145732
  7.2 5.8 %copy-start.4 = (bf16[128,1,128]{2,0,1:T(8,128)(2,1)S(1)}, bf16[128,1,128]{2,0,1:T(8,128)(2,1)}, u32[]{:S(2)}) copy-start(bf16[128,1,128]{2,0,1:T(8,128)(2,1)} %param.19) | copy-start | bytes 98308
  7.2 48.0 %reduce-scatter.2.cloned.1.call-start = ((), (), s32[]{:S(2)}) async-start(), calls=%async_computation.3 | async-start | bytes 1179648 | tf_op jit(solution)/shard_map/reduce_scatter | solution.py:57
  13.5 4.0 %copy-start.6 = (s32[16,8]{0,1:T(8,128)S(1)}, s32[16,8]{0,1:T(8,128)}, u32[]{:S(2)}) copy-start(s32[16,8]{0,1:T(8,128)} %param.25) | copy-start | bytes 1540
  13.5 4.0 %copy-start.7 = (s32[16,8]{0,1:T(8,128)S(1)}, s32[16,8]{0,1:T(8,128)}, u32[]{:S(2)}) copy-start(s32[16,8]{0,1:T(8,128)} %param.24) | copy-start | bytes 1540
  13.5 41.6 %copy-start.3 = (bf16[16,4096]{1,0:T(8,128)(2,1)S(1)}, bf16[16,4096]{1,0:T(8,128)(2,1)}, u32[]{:S(2)}) copy-start(bf16[16,4096]{1,0:T(8,128)(2,1)} %param.22) | copy-start | bytes 393220
  13.6 42.7 %copy-start.5 = (f32[4096]{0:T(1024)S(1)}, f32[4096]{0:T(1024)}, u32[]{:S(2)}) copy-start(f32[4096]{0:T(1024)} %param.23) | copy-start | bytes 49156
  56.1 5.7 %copy-start.2 = (bf16[16,4096]{1,0:T(8,128)(2,1)}, bf16[16,4096]{1,0:T(8,128)(2,1)S(1)}, u32[]{:S(2)}) copy-start(bf16[16,4096]{1,0:T(8,128)(2,1)S(1)} %add_convert_fusion) | copy-start | bytes 393220
  100.2 6.3 %copy-start.1 = (bf16[256,4096]{1,0:T(8,128)(2,1)S(1)}, bf16[256,4096]{1,0:T(8,128)(2,1)}, u32[]{:S(2)}) copy-start(bf16[256,4096]{1,0:T(8,128)(2,1)} %reshape.95) | copy-start | bytes 6291460
  121.6 6.5 %copy-start.8 = (f32[16,8]{0,1:T(8,128)S(1)}, f32[16,8]{0,1:T(8,128)}, u32[]{:S(2)}) copy-start(f32[16,8]{0,1:T(8,128)} %param.26) | copy-start | bytes 1540
  121.6 34.8 %all-to-all-start.1 = ((bf16[128,2,4096]{2,1,0:T(2,128)(2,1)}), bf16[128,2,4096]{2,1,0:T(2,128)(2,1)}, u32[]{:S(2)}, u32[]{:S(2)}) async-start(bf16[128,2,4096]{2,1,0:T(2,128)(2,1)} %reshape.96), calls=%async_computation.2 | async-start | bytes 4194304 | tf_op jit(solution)/shard_map/all_to_all | solution.py:89
Sparse Core Ops, SparseCore 0:
  17.7 37.4 reduce-scatter.1
where the time goes:
time: 171 us
  waiting for transfers between devices  65.6 us (38%)
  blocking collectives  36.2 us (21%)
  matrix products  24.4 us (14%)
  local copies, waits for them, and re-layouts  18.8 us (11%)
  between operations  14.2 us (8%)
  starting transfers between devices  6.55 us (4%)
  other arithmetic  5.05 us (3%)
    reduce_scatter x1, waiting for transfers between devices, on_device(): lax.psum_scatter(jnp.dot(attn, out_proj, preferred_element_type=jnp.float...  37.4 us
    all_to_all x1, blocking collectives, on_device(): lax.all_to_all(outgoing.reshape(expert_count, capacity, width), ('sec', '...  36.2 us
    all_to_all x1, waiting for transfers between devices, on_device(): lax.all_to_all(finished.reshape(arrived.shape), ('sec', 'req', 'kv'), spl...  28.2 us
    dot_general x1, matrix products, on_device(): jnp.dot(hidden, w_down[0], preferred_element_type=jnp.float32)  10.7 us
    all_to_all x1, starting transfers between devices, on_device(): lax.all_to_all(finished.reshape(arrived.shape), ('sec', 'req', 'kv'), spl...  6.51 us
    dot_general x1, matrix products, on_device(): gate_out = jnp.dot(flat_rows, w_gate[0], preferred_element_type=jnp.float32)  6.26 us
    reshape x1, local copies, waits for them, and re-layouts, on_device(): finished.reshape(arrived.shape)  4.4 us
    dot_general x1, matrix products, on_device(): jnp.dot(attn, out_proj, preferred_element_type=jnp.float32)  3.94 us
  transfers between devices with their start and end apart: 2, of which 2 were waited for; matrix products, arithmetic and copies ran while one was open for 0% of the time, Pallas kernels for 0%

commit v1 on v0

v1 whole, which is shorter than its diff:
```python
import jax
import jax.numpy as jnp
from jax import lax
from jax.experimental import pallas as pl
from jax.experimental.pallas import tpu as pltpu
from jax.sharding import PartitionSpec as P

LANES = 128
F32 = jnp.float32
BF16 = jnp.bfloat16
MIB = 1 << 20

VMEM = pltpu.VMEM
SMEM = pltpu.SMEM


def whole(space=VMEM):
    return pl.BlockSpec(memory_space=space)


def attend_kernel(sec_ref, q_ref, kc_ref, vc_ref, nk_ref, nv_ref, len_ref, wo_ref, theirs_ref, mine_ref, attn_ref):
    rows, head_width = q_ref.shape
    heads = head_width // LANES
    positions = kc_ref.shape[0] // rows
    group = 16
    scale = 1.0 / LANES**0.5
    half = rows // 2

    @pl.when(pl.program_id(0) == 0)
    def _():
        r = lax.broadcasted_iota(jnp.int32, (rows, rows), 0)
        c = lax.broadcasted_iota(jnp.int32, (rows, rows), 1)
        lengths = jnp.sum(jnp.where(r == c, len_ref[...], 0).astype(F32), axis=1, keepdims=True)
        span = group * positions
        row_token = lax.broadcasted_iota(jnp.int32, (heads * group, span), 0) % group
        column = lax.broadcasted_iota(jnp.int32, (heads * group, span), 1)
        own_column = column - row_token * positions
        own_position = jnp.where(own_column >= 0, own_column, positions).astype(F32)
        for g in range(rows // group):
            at = pl.ds(g * group, group)
            q = jnp.concatenate([q_ref[at, pl.ds(h * LANES, LANES)] for h in range(heads)], axis=0)
            keys = kc_ref[pl.ds(g * span, span), :]
            score = lax.dot_general(q, keys, (((1,), (1,)), ((), ())), preferred_element_type=F32) * scale
            new_key = jnp.concatenate([nk_ref[at, :].astype(F32)] * heads, axis=0)
            own_score = jnp.sum(q.astype(F32) * new_key, axis=1, keepdims=True) * scale
            limit = jnp.concatenate([lengths[g * group : (g + 1) * group]] * heads, axis=0)
            score = jnp.where(own_position < limit, score, -jnp.inf)
            highest = jnp.maximum(jnp.max(score, axis=1, keepdims=True), own_score)
            raised = jnp.exp(score - highest)
            own_raised = jnp.exp(own_score - highest)
            inverse = 1.0 / (jnp.sum(raised, axis=1, keepdims=True) + own_raised)
            weight = (raised * inverse).astype(BF16)
            own_weight = (own_raised * inverse).astype(BF16).astype(F32)
            values = vc_ref[pl.ds(g * span, span), :]
            out = jnp.dot(weight, values, preferred_element_type=F32)
            out = out + own_weight * jnp.concatenate([nv_ref[at, :].astype(F32)] * heads, axis=0)
            out = out.astype(BF16)
            place = lax.rem(g * group + half * (1 - sec_ref[0]), rows)
            place = pl.multiple_of(place, group)
            for h in range(heads):
                attn_ref[pl.ds(place, group), pl.ds(h * LANES, LANES)] = out[h * group : (h + 1) * group]

    proj = jnp.dot(attn_ref[...], wo_ref[...], preferred_element_type=F32)
    theirs_ref[...] = proj[:half].astype(BF16)
    mine_ref[...] = proj[half:].astype(BF16)


def attend(sec, q, kc, vc, nk, nv, lengths, wo):
    rows, head_width = q.shape
    width = wo.shape[1]
    steps = 4
    block = width // steps
    full = lambda a: pl.BlockSpec(a.shape, lambda i, s: (0, 0))
    out = jax.ShapeDtypeStruct((rows // 2, width), BF16)
    out_spec = pl.BlockSpec((rows // 2, block), lambda i, s: (0, i))
    return pl.pallas_call(
        attend_kernel,
        grid_spec=pltpu.PrefetchScalarGridSpec(
            num_scalar_prefetch=1,
            grid=(steps,),
            in_specs=[full(a) for a in (q, kc, vc, nk, nv, lengths)] + [pl.BlockSpec((head_width, block), lambda i, s: (0, i))],
            out_specs=[out_spec, out_spec],
            scratch_shapes=[pltpu.VMEM((rows, head_width), BF16)],
        ),
        out_shape=[out, out],
        compiler_params=pltpu.CompilerParams(vmem_limit_bytes=24 * MIB),
        name="attend",
    )(sec, q, kc, vc, nk, nv, lengths, wo)


def quarter_kernel(kv_ref, mine_ref, got_ref, *out_refs):
    count = len(out_refs)
    rows = mine_ref.shape[0] // count
    for step, out_ref in enumerate(out_refs):
        at = pl.ds(pl.multiple_of(lax.rem(kv_ref[0] + step, count) * rows, rows), rows)
        out_ref[...] = (mine_ref[at, :].astype(F32) + got_ref[at, :].astype(F32)).astype(BF16)


def quarter(kv, mine, got, count):
    rows, width = mine.shape
    out = jax.ShapeDtypeStruct((rows // count, width), BF16)
    return pl.pallas_call(
        quarter_kernel,
        in_specs=[whole(SMEM), whole(), whole()],
        out_specs=[whole()] * count,
        out_shape=[out] * count,
        name="quarter",
    )(kv, mine, got)


def route_kernel(ids_ref, slots_ref, *refs):
    part_refs, (residual_ref, gain_ref, stream_ref, out_ref, wide_ref, row_ref) = refs[:-6], refs[-6:]
    rows, width = residual_ref.shape
    pieces = width // LANES
    top = ids_ref.shape[0]
    capacity = out_ref.shape[1]
    out_ref[...] = jnp.zeros_like(out_ref)
    proj = part_refs[0][...].astype(F32)
    for part_ref in part_refs[1:]:
        proj = proj + part_ref[...].astype(F32)
    stream = (residual_ref[...].astype(F32) + proj).astype(BF16)
    stream_ref[...] = stream
    widened = stream.astype(F32)
    mean_square = jnp.mean(widened * widened, axis=-1, keepdims=True)
    normed = widened * lax.rsqrt(mean_square + 1e-06) * gain_ref[...]
    for t in range(0, rows, 8):
        for s in range(pieces):
            wide_ref[pl.ds(t * pieces + s, 8, stride=pieces), :] = normed[t : t + 8, s * LANES : (s + 1) * LANES]
    row_ref[...] = wide_ref[...].astype(BF16).reshape(rows, pieces, LANES)

    def one(t, carry):
        row = row_ref[t]
        for k in range(top):
            out_ref[ids_ref[k, t], slots_ref[k, t]] = row
        return carry

    lax.fori_loop(0, rows, one, 0)


def route(ids, slots, parts, residual, gain, expert_count, capacity):
    rows, width = residual.shape
    pieces = width // LANES
    return pl.pallas_call(
        route_kernel,
        in_specs=[whole(SMEM), whole(SMEM)] + [whole()] * (len(parts) + 2),
        out_specs=[whole(), whole()],
        out_shape=[
            jax.ShapeDtypeStruct((rows, width), BF16),
            jax.ShapeDtypeStruct((expert_count, capacity, pieces, LANES), BF16),
        ],
        scratch_shapes=[pltpu.VMEM((rows * pieces, LANES), F32), pltpu.VMEM((rows, pieces, LANES), BF16)],
        compiler_params=pltpu.CompilerParams(vmem_limit_bytes=16 * MIB),
        name="route",
    )(ids, slots, *parts, residual, gain)


def expert_kernel(x_ref, wg_ref, wu_ref, wd_ref, out_ref, wide_ref, flat_ref, wg, wu, wd, hidden_ref, in_sems, down_sems):
    rows, pieces, _ = x_ref.shape
    hidden_width = wg_ref.shape[1]
    width = pieces * LANES
    ncols = 256
    nsteps = hidden_width // ncols
    dsteps = down_sems.shape[0]
    dcols = width // dsteps

    def gate_copies(n):
        at = pl.ds(n * ncols, ncols)
        return (
            pltpu.make_async_copy(wg_ref.at[:, at], wg.at[n], in_sems.at[0, n]),
            pltpu.make_async_copy(wu_ref.at[:, at], wu.at[n], in_sems.at[1, n]),
        )

    def down_copy(n):
        return pltpu.make_async_copy(wd_ref.at[:, pl.ds(n * dcols, dcols)], wd.at[n], down_sems.at[n])

    for n in range(nsteps):
        for copy in gate_copies(n):
            copy.start()
    for n in range(dsteps):
        down_copy(n).start()

    group = 16

    def spread(i, carry):
        base = pl.multiple_of(i * group, group)
        wide_ref[pl.ds(0, group * pieces), :] = x_ref[pl.ds(base, group)].reshape(group * pieces, LANES).astype(F32)
        for s in range(pieces):
            low = wide_ref[pl.ds(s, 8, stride=pieces), :]
            high = wide_ref[pl.ds(8 * pieces + s, 8, stride=pieces), :]
            flat_ref[pl.ds(base, group), pl.ds(s * LANES, LANES)] = jnp.concatenate([low, high], axis=0).astype(BF16)
        return carry

    lax.fori_loop(0, rows // group, spread, 0)

    for n in range(nsteps):
        for copy in gate_copies(n):
            copy.wait()
        gate = jnp.dot(flat_ref[...], wg[n], preferred_element_type=F32)
        up = jnp.dot(flat_ref[...], wu[n], preferred_element_type=F32)
        hidden_ref[:, pl.ds(n * ncols, ncols)] = (gate / (1.0 + jnp.exp(-gate)) * up).astype(BF16)

    for n in range(dsteps):
        down_copy(n).wait()
        done = jnp.dot(hidden_ref[...], wd[n], preferred_element_type=F32)
        for r in range(0, rows, 8):
            for s in range(dcols // LANES):
                wide_ref[pl.ds(r * pieces + n * (dcols // LANES) + s, 8, stride=pieces), :] = done[
                    r : r + 8, s * LANES : (s + 1) * LANES
                ]

    def narrow(i, carry):
        base = pl.multiple_of(i * group, group)
        at = pl.ds(pl.multiple_of(i * group * pieces, group * pieces), group * pieces)
        out_ref[pl.ds(base, group)] = wide_ref[at, :].astype(BF16).reshape(group, pieces, LANES)
        return carry

    lax.fori_loop(0, rows // group, narrow, 0)


def expert(x, wg, wu, wd):
    rows, pieces, _ = x.shape
    width, hidden_width = wg.shape
    nsteps, dsteps = hidden_width // 256, 4
    return pl.pallas_call(
        expert_kernel,
        in_specs=[whole()] + [pl.BlockSpec(memory_space=pl.ANY)] * 3,
        out_specs=whole(),
        out_shape=jax.ShapeDtypeStruct(x.shape, BF16),
        scratch_shapes=[
            pltpu.VMEM((rows * pieces, LANES), F32),
            pltpu.VMEM((rows, width), BF16),
            pltpu.VMEM((nsteps, width, 256), BF16),
            pltpu.VMEM((nsteps, width, 256), BF16),
            pltpu.VMEM((dsteps, hidden_width, width // dsteps), BF16),
            pltpu.VMEM((rows, hidden_width), BF16),
            pltpu.SemaphoreType.DMA((2, nsteps)),
            pltpu.SemaphoreType.DMA((dsteps,)),
        ],
        compiler_params=pltpu.CompilerParams(vmem_limit_bytes=44 * MIB),
        name="expert",
    )(x, wg, wu, wd)


def combine_kernel(ids_ref, slots_ref, probs_ref, rows_ref, out_ref, wide_ref):
    rows, width = out_ref.shape
    pieces = width // LANES
    top = ids_ref.shape[0]

    def one(t, carry):
        total = None
        for k in range(top):
            term = rows_ref[ids_ref[k, t], slots_ref[k, t]].astype(F32) * probs_ref[k, t]
            total = term if total is None else total + term
        wide_ref[pl.ds(pl.multiple_of(t * pieces, pieces), pieces), :] = total
        return carry

    lax.fori_loop(0, rows, one, 0)
    for s in range(pieces):
        low = wide_ref[pl.ds(s, 8, stride=pieces), :]
        high = wide_ref[pl.ds(8 * pieces + s, 8, stride=pieces), :]
        out_ref[:, pl.ds(s * LANES, LANES)] = jnp.concatenate([low, high], axis=0).astype(BF16)


def combine(ids, slots, probs, returned, width):
    rows = ids.shape[1]
    return pl.pallas_call(
        combine_kernel,
        in_specs=[whole(SMEM)] * 3 + [whole()],
        out_specs=whole(),
        out_shape=jax.ShapeDtypeStruct((rows, width), BF16),
        scratch_shapes=[pltpu.VMEM((rows * width // LANES, LANES), F32)],
        compiler_params=pltpu.CompilerParams(vmem_limit_bytes=16 * MIB),
        name="combine",
    )(ids, slots, probs, returned)


def on_device(
    queries,
    key_cache,
    value_cache,
    new_keys,
    new_values,
    lengths,
    out_proj,
    residual,
    norm_gain,
    expert_ids,
    expert_slots,
    gate_probs,
    w_gate,
    w_up,
    w_down,
):
    row_count = queries.shape[0]
    width = out_proj.shape[1]
    pieces = width // LANES
    sec_count, group_count = lax.axis_size("sec"), lax.axis_size("kv")
    expert_count = sec_count * lax.axis_size("req") * group_count
    row_share, top_count = expert_ids.shape
    capacity = top_count * row_share // expert_count + 1
    sec = lax.axis_index("sec").astype(jnp.int32).reshape(1)
    kv = lax.axis_index("kv").astype(jnp.int32).reshape(1)

    theirs, mine = attend(
        sec,
        queries,
        key_cache.reshape(-1, LANES),
        value_cache.reshape(-1, LANES),
        new_keys.reshape(row_count, LANES),
        new_values.reshape(row_count, LANES),
        lengths.reshape(1, row_count),
        out_proj,
    )
    got = lax.ppermute(theirs, "sec", [(i, 1 - i) for i in range(sec_count)])
    quarters = quarter(kv, mine, got, group_count)
    parts = [quarters[0]] + [
        lax.ppermute(quarters[s], "kv", [(i, (i + s) % group_count) for i in range(group_count)])
        for s in range(1, group_count)
    ]
    ids, slots, probs = expert_ids.T, expert_slots.T, gate_probs.T
    stream, outgoing = route(ids, slots, parts, residual, norm_gain.reshape(1, width), expert_count, capacity)

    def exchange(rows):
        sent = rows.reshape(expert_count, capacity * pieces, LANES)
        return lax.all_to_all(sent, ("sec", "req", "kv"), split_axis=0, concat_axis=0, tiled=True)

    arrived = exchange(outgoing).reshape(expert_count * capacity, pieces, LANES)
    finished = expert(arrived, w_gate[0], w_up[0], w_down[0])
    returned = exchange(finished).reshape(expert_count, capacity, pieces, LANES)
    moe_out = combine(ids, slots, probs, returned, width)
    return (stream, moe_out)


def solution(mesh):
    return jax.shard_map(
        on_device,
        mesh=mesh,
        in_specs=(
            P("req", ("kv", "sec")),
            P("req", "kv", None, None),
            P("req", "kv", None, None),
            P("req", "kv", None),
            P("req", "kv", None),
            P("req"),
            P(("kv", "sec"), None),
            P(("req", "sec", "kv"), None),
            P(),
            P(("req", "sec", "kv"), None),
            P(("req", "sec", "kv"), None),
            P(("req", "sec", "kv"), None),
            P(("sec", "req", "kv"), None, None),
            P(("sec", "req", "kv"), None, None),
            P(("sec", "req", "kv"), None, None),
        ),
        out_specs=(P(("req", "sec", "kv"), None), P(("req", "sec", "kv"), None)),
        check_vma=False,
    )
```

time: 171 us -> 121 us (0.71)
  waiting for transfers between devices: 65.6 us -> 6.64 us
  blocking collectives: 36.2 us -> 73.7 us
  matrix products: 24.4 us -> 0 us
  Pallas kernels: 0 us -> 23 us
  between operations: 14.2 us -> 0.74 us
  local copies, waits for them, and re-layouts: 18.8 us -> 10.2 us
  other arithmetic: 5.05 us -> 0 us
    all_to_all x1 -> x2, blocking collectives: 36.2 us -> 73.7 us  [exchange(): lax.all_to_all(sent, ('sec', 'req', 'kv'), split_axis=0, concat_axis=0, t...]
    reduce_scatter x1 -> x0, waiting for transfers between devices: 37.4 us -> none  [on_device(): lax.psum_scatter(jnp.dot(attn, out_proj, preferred_element_type=jnp.float...]
    all_to_all x1 -> x0, waiting for transfers between devices: 28.2 us -> none  [on_device(): lax.all_to_all(finished.reshape(arrived.shape), ('sec', 'req', 'kv'), spl...]
    dot_general x6 -> x0, matrix products: 24.4 us -> none  [the longest x1 10.7 us: on_device(): jnp.dot(hidden, w_down[0], preferred_element_type=jnp.float32)]
    pallas_call x0 -> x5, Pallas kernels: none -> 23 us  [the longest x1 12 us: expert(): pl.pallas_call(expert_kernel, in_specs=[whole()] + [pl.BlockSpec(memory_s...]
    reshape x6 -> x0, local copies, waits for them, and re-layouts: 13.1 us -> none  [the longest x1 4.4 us: on_device(): finished.reshape(arrived.shape)]
    unnamed x19 -> x30, local copies, waits for them, and re-layouts: 0.13 us -> 10.2 us
    ppermute x0 -> x4, waiting for transfers between devices: none -> 6.64 us  [the longest x3 5.1 us: on_device(): lax.ppermute(quarters[s], 'kv', [(i, (i + s) % group_count) for i in rang...]
  transfers between devices with their start and end apart: 2 -> 4, of which waited for: 2 -> 3; matrix products, arithmetic and copies ran while one was open for 0% -> 0% of each run, Pallas kernels for 0% -> 0%
where the time goes in v1:
time: 121 us
  blocking collectives  73.7 us (61%)
  Pallas kernels  23 us (19%)
  local copies, waits for them, and re-layouts  10.2 us (8%)
  waiting for transfers between devices  6.64 us (5%)
  starting transfers between devices  6.33 us (5%)
    all_to_all x2, blocking collectives, exchange(): lax.all_to_all(sent, ('sec', 'req', 'kv'), split_axis=0, concat_axis=0, t...  73.7 us
    pallas_call x1, Pallas kernels, expert(): pl.pallas_call(expert_kernel, in_specs=[whole()] + [pl.BlockSpec(memory_s...  12 us
    unnamed x30, local copies, waits for them, and re-layouts  10.2 us
    ppermute x3, waiting for transfers between devices, on_device(): lax.ppermute(quarters[s], 'kv', [(i, (i + s) % group_count) for i in rang...  5.1 us
    ppermute x3, starting transfers between devices, on_device(): lax.ppermute(quarters[s], 'kv', [(i, (i + s) % group_count) for i in rang...  4.91 us
    pallas_call x1, Pallas kernels, attend(): pl.pallas_call(attend_kernel, grid_spec=pltpu.PrefetchScalarGridSpec(num_...  4.51 us
    pallas_call x1, Pallas kernels, route(): pl.pallas_call(route_kernel, in_specs=[whole(SMEM), whole(SMEM)] + [whole...  2.46 us
  transfers between devices with their start and end apart: 4, of which 3 were waited for; matrix products, arithmetic and copies ran while one was open for 0% of the time, Pallas kernels for 0%

profile of v1, /device:TPU:1, one launch (start us, length us, event | category | flops | bytes accessed | tf_op | source)
XLA Modules:
  0.0 120.6 jit_solution(12207723236691971559)
XLA Ops:
  0.6 0.0 copy-start.10
  0.6 0.0 copy-start.9
  0.7 0.0 copy-start
  0.7 2.2 %copy-done = bf16[512,4096]{1,0:T(8,128)(2,1)S(1)} copy-done((bf16[512,4096]{1,0:T(8,128)(2,1)S(1)}, bf16[512,4096]{1,0:T(8,128)(2,1)}, u32[]{:S(2)}) %copy-start) | copy-done | bytes 4194328
  2.9 0.0 copy-start.1
  2.9 1.2 %copy-done.1 = bf16[128,1,32,128]{3,2,1,0:T(8,128)(2,1)S(1)} copy-done((bf16[128,1,32,128]{3,2,1,0:T(8,128)(2,1)S(1)}, bf16[128,1,32,128]{3,2,1,0:T(8,128)(2,1)}, u32[]{:S(2)}) %copy-start.1) | copy-done | bytes 1048600
  4.1 0.0 copy-start.2
  4.1 1.2 %copy-done.2 = bf16[128,1,32,128]{3,2,1,0:T(8,128)(2,1)S(1)} copy-done((bf16[128,1,32,128]{3,2,1,0:T(8,128)(2,1)S(1)}, bf16[128,1,32,128]{3,2,1,0:T(8,128)(2,1)}, u32[]{:S(2)}) %copy-start.2) | copy-done | bytes 1048600
  5.3 0.0 copy-start.4
  5.3 0.9 copy-done.4
  6.2 0.0 copy-start.7
  6.2 0.8 copy-done.7
  7.0 0.0 copy-start.8
  7.0 0.8 copy-done.8
  7.7 0.0 copy-start.13
  7.7 0.7 copy-done.13
  8.4 0.0 copy-start.5
  8.4 0.0 copy-start.11
  8.4 4.5 %attend.1 = (bf16[64,4096]{1,0:T(8,128)(2,1)S(1)}, bf16[64,4096]{1,0:T(8,128)(2,1)S(1)}) custom-call(s32[1]{0:T(128)} %bitcast.3.sec_ref, bf16[128,512]{1,0:T(8,128)(2,1)S(1)} %copy-done.4, bf16[4096,128]{1,0:T(8,128)(2,1)S(1)} %bitcast.22, bf16[4096,128]{1,0:T(8,128)(2,1)S(1)} %bitcast.23, bf16[128,128]{1,0:T(8,128)(2,1)S(1)} %bitcast.24, ...), custom_call_target="tpu_custom_call" | custom-call | tf_op jit(solution)/shard_map/attend/pallas_call | solution.py:76
  12.9 0.0 copy-start.3
  12.9 0.8 copy-done.3
  13.7 1.4 %collective-permute-start = (bf16[64,4096]{1,0:T(8,128)(2,1)S(1)}, bf16[64,4096]{1,0:T(8,128)(2,1)S(1)}, u32[]{:S(2)}, u32[]{:S(2)}) collective-permute-start(bf16[64,4096]{1,0:T(8,128)(2,1)S(1)} %get-tuple-element.11), channel_id=1, source_target_pairs={{0,64},{64,0},{1,65},{65,1},{2,66},{66,2},{3,67},{67,3},{4,68},{68... | collective-permute-start | bytes 1572872 | tf_op jit(solution)/shard_map/ppermute | solution.py:314
  15.1 1.5 %collective-permute-done.got_ref = bf16[64,4096]{1,0:T(8,128)(2,1)S(1)} collective-permute-done((bf16[64,4096]{1,0:T(8,128)(2,1)S(1)}, bf16[64,4096]{1,0:T(8,128)(2,1)S(1)}, u32[]{:S(2)}, u32[]{:S(2)}) %collective-permute-start) | collective-permute-done | bytes 524320 | tf_op jit(solution)/shard_map/ppermute | solution.py:314
  16.7 0.0 copy-start.14
  16.7 0.8 copy-done.14
  17.4 2.0 %quarter.1 = (bf16[16,4096]{1,0:T(8,128)(2,1)}, bf16[16,4096]{1,0:T(8,128)(2,1)}, bf16[16,4096]{1,0:T(8,128)(2,1)}, bf16[16,4096]{1,0:T(8,128)(2,1)}) custom-call(s32[1]{0:T(128)} %bitcast.2.kv_ref, bf16[64,4096]{1,0:T(8,128)(2,1)} %copy-done.3, bf16[64,4096]{1,0:T(8,128)(2,1)} %copy-done.14), custom_call_target="tpu_custom_call" | custom-call | tf_op jit(solution)/shard_map/quarter/pallas_call | solution.py:102
  19.5 1.3 %collective-permute-start.1 = (bf16[16,4096]{1,0:T(8,128)(2,1)}, bf16[16,4096]{1,0:T(8,128)(2,1)S(1)}, u32[]{:S(2)}, u32[]{:S(2)}) collective-permute-start(bf16[16,4096]{1,0:T(8,128)(2,1)} %get-tuple-element.13), channel_id=1, source_target_pairs={{0,1},{1,2},{2,3},{3,0},{4,5},{5,6},{6,7},{7,4},{8,9},{9,10},{10,1... | collective-permute-start | bytes 393224 | tf_op jit(solution)/shard_map/ppermute | solution.py:317
  20.8 2.5 %collective-permute-start.2 = (bf16[16,4096]{1,0:T(8,128)(2,1)}, bf16[16,4096]{1,0:T(8,128)(2,1)S(1)}, u32[]{:S(2)}, u32[]{:S(2)}) collective-permute-start(bf16[16,4096]{1,0:T(8,128)(2,1)} %get-tuple-element.14), channel_id=1, source_target_pairs={{0,2},{1,3},{2,0},{3,1},{4,6},{5,7},{6,4},{7,5},{8,10},{9,11},{10,... | collective-permute-start | bytes 393224 | tf_op jit(solution)/shard_map/ppermute | solution.py:317
  23.2 1.2 collective-permute-start.3
  24.4 1.2 %collective-permute-done.1.refs_1_ = bf16[16,4096]{1,0:T(8,128)(2,1)S(1)} collective-permute-done((bf16[16,4096]{1,0:T(8,128)(2,1)}, bf16[16,4096]{1,0:T(8,128)(2,1)S(1)}, u32[]{:S(2)}, u32[]{:S(2)}) %collective-permute-start.1) | collective-permute-done | bytes 131104 | tf_op jit(solution)/shard_map/ppermute | solution.py:317
  25.6 3.9 %collective-permute-done.2.refs_2_ = bf16[16,4096]{1,0:T(8,128)(2,1)S(1)} collective-permute-done((bf16[16,4096]{1,0:T(8,128)(2,1)}, bf16[16,4096]{1,0:T(8,128)(2,1)S(1)}, u32[]{:S(2)}, u32[]{:S(2)}) %collective-permute-start.2) | collective-permute-done | bytes 131104 | tf_op jit(solution)/shard_map/ppermute | solution.py:317
  29.5 0.0 collective-permute-done.3.refs_3_
  29.5 0.0 copy-done.10
  29.5 0.0 copy-done.9
  29.5 0.0 copy-done.5
  29.5 0.0 copy-done.11
  29.5 0.0 copy-start.6
  29.5 0.9 copy-done.6
  30.4 2.5 %route.1 = (bf16[16,4096]{1,0:T(8,128)(2,1)}, bf16[128,2,32,128]{3,2,1,0:T(8,128)(2,1)S(1)}) custom-call(s32[8,16]{1,0:T(8,128)S(1)} %bitcast.26, s32[8,16]{1,0:T(8,128)S(1)} %bitcast.28, bf16[16,4096]{1,0:T(8,128)(2,1)S(1)} %copy-done.6, bf16[16,4096]{1,0:T(8,128)(2,1)S(1)} %collective-permute-done.1.refs_1_, ...), custom_call_target="tpu_custom_call" | custom-call | tf_op jit(solution)/shard_map/route/pallas_call | solution.py:143
  32.9 39.2 %all_to_all.10 = bf16[128,64,128]{2,1,0:T(8,128)(2,1)S(1)} all-to-all(bf16[128,64,128]{2,1,0:T(8,128)(2,1)S(1)} %bitcast.21), channel_id=1, replica_groups=mesh['sec'=2,'req'=16,'kv'=4] {'sec','req','kv'}, dimensions={0} | all-to-all | bytes 4194304 | tf_op jit(solution)/shard_map/all_to_all | solution.py:325
  72.1 12.0 %expert.1 = bf16[256,32,128]{2,1,0:T(8,128)(2,1)S(1)} custom-call(bf16[256,32,128]{2,1,0:T(8,128)(2,1)S(1)} %bitcast.19, bf16[4096,768]{1,0:T(8,128)(2,1)} %bitcast.33, bf16[4096,768]{1,0:T(8,128)(2,1)} %bitcast.34, bf16[768,4096]{1,0:T(8,128)(2,1)} %bitcast.35), custom_call_target="tpu_custom_call" | custom-call | tf_op jit(solution)/shard_map/expert/pallas_call | solution.py:224
  84.1 0.0 copy-start.12
  84.1 34.5 %all_to_all.11 = bf16[128,64,128]{2,1,0:T(8,128)(2,1)S(1)} all-to-all(bf16[128,64,128]{2,1,0:T(8,128)(2,1)S(1)} %bitcast.20), channel_id=1, replica_groups=mesh['sec'=2,'req'=16,'kv'=4] {'sec','req','kv'}, dimensions={0} | all-to-all | bytes 4194304 | tf_op jit(solution)/shard_map/all_to_all | solution.py:325
  118.6 0.0 copy-done.12
  118.6 2.0 %combine.1 = bf16[16,4096]{1,0:T(8,128)(2,1)} custom-call(s32[8,16]{1,0:T(8,128)S(1)} %bitcast.27, s32[8,16]{1,0:T(8,128)S(1)} %bitcast.29, f32[8,16]{1,0:T(8,128)S(1)} %bitcast.31, bf16[128,2,32,128]{3,2,1,0:T(8,128)(2,1)S(1)} %bitcast.18), custom_call_target="tpu_custom_call" | custom-call | tf_op jit(solution)/shard_map/combine/pallas_call | solution.py:266
Async XLA Ops:
  0.6 28.8 %copy-start.10 = (s32[16,8]{0,1:T(8,128)S(1)}, s32[16,8]{0,1:T(8,128)}, u32[]{:S(2)}) copy-start(s32[16,8]{0,1:T(8,128)} %param.25) | copy-start | bytes 1540
  0.6 28.8 %copy-start.9 = (s32[16,8]{0,1:T(8,128)S(1)}, s32[16,8]{0,1:T(8,128)}, u32[]{:S(2)}) copy-start(s32[16,8]{0,1:T(8,128)} %param.24) | copy-start | bytes 1540
  0.7 2.2 %copy-start = (bf16[512,4096]{1,0:T(8,128)(2,1)S(1)}, bf16[512,4096]{1,0:T(8,128)(2,1)}, u32[]{:S(2)}) copy-start(bf16[512,4096]{1,0:T(8,128)(2,1)} %wo_ref.1) | copy-start | bytes 12582916
  2.9 1.2 %copy-start.1 = (bf16[128,1,32,128]{3,2,1,0:T(8,128)(2,1)S(1)}, bf16[128,1,32,128]{3,2,1,0:T(8,128)(2,1)}, u32[]{:S(2)}) copy-start(bf16[128,1,32,128]{3,2,1,0:T(8,128)(2,1)} %param.16) | copy-start | bytes 3145732
  4.1 1.2 %copy-start.2 = (bf16[128,1,32,128]{3,2,1,0:T(8,128)(2,1)S(1)}, bf16[128,1,32,128]{3,2,1,0:T(8,128)(2,1)}, u32[]{:S(2)}) copy-start(bf16[128,1,32,128]{3,2,1,0:T(8,128)(2,1)} %param.17) | copy-start | bytes 3145732
  5.3 0.9 copy-start.4
  6.2 0.8 copy-start.7
  7.0 0.8 copy-start.8
  7.7 0.7 copy-start.13
  8.4 21.1 %copy-start.5 = (bf16[16,4096]{1,0:T(8,128)(2,1)S(1)}, bf16[16,4096]{1,0:T(8,128)(2,1)}, u32[]{:S(2)}) copy-start(bf16[16,4096]{1,0:T(8,128)(2,1)} %refs_4_.1) | copy-start | bytes 393220
  8.4 21.1 %copy-start.11 = (f32[4096]{0:T(1024)S(1)}, f32[4096]{0:T(1024)}, u32[]{:S(2)}) copy-start(f32[4096]{0:T(1024)} %param.23) | copy-start | bytes 49156
  12.9 0.8 copy-start.3
  13.7 3.0 %collective-permute-start = (bf16[64,4096]{1,0:T(8,128)(2,1)S(1)}, bf16[64,4096]{1,0:T(8,128)(2,1)S(1)}, u32[]{:S(2)}, u32[]{:S(2)}) collective-permute-start(bf16[64,4096]{1,0:T(8,128)(2,1)S(1)} %get-tuple-element.11), channel_id=1, source_target_pairs={{0,64},{64,0},{1,65},{65,1},{2,66},{66,2},{3,67},{67,3},{4,68},{68... | collective-permute-start | bytes 1572872 | tf_op jit(solution)/shard_map/ppermute | solution.py:314
  16.7 0.8 copy-start.14
  19.5 6.1 %collective-permute-start.1 = (bf16[16,4096]{1,0:T(8,128)(2,1)}, bf16[16,4096]{1,0:T(8,128)(2,1)S(1)}, u32[]{:S(2)}, u32[]{:S(2)}) collective-permute-start(bf16[16,4096]{1,0:T(8,128)(2,1)} %get-tuple-element.13), channel_id=1, source_target_pairs={{0,1},{1,2},{2,3},{3,0},{4,5},{5,6},{6,7},{7,4},{8,9},{9,10},{10,1... | collective-permute-start | bytes 393224 | tf_op jit(solution)/shard_map/ppermute | solution.py:317
  20.8 8.7 %collective-permute-start.2 = (bf16[16,4096]{1,0:T(8,128)(2,1)}, bf16[16,4096]{1,0:T(8,128)(2,1)S(1)}, u32[]{:S(2)}, u32[]{:S(2)}) collective-permute-start(bf16[16,4096]{1,0:T(8,128)(2,1)} %get-tuple-element.14), channel_id=1, source_target_pairs={{0,2},{1,3},{2,0},{3,1},{4,6},{5,7},{6,4},{7,5},{8,10},{9,11},{10,... | collective-permute-start | bytes 393224 | tf_op jit(solution)/shard_map/ppermute | solution.py:317
  23.2 6.3 %collective-permute-start.3 = (bf16[16,4096]{1,0:T(8,128)(2,1)}, bf16[16,4096]{1,0:T(8,128)(2,1)S(1)}, u32[]{:S(2)}, u32[]{:S(2)}) collective-permute-start(bf16[16,4096]{1,0:T(8,128)(2,1)} %get-tuple-element.15), channel_id=1, source_target_pairs={{0,3},{1,0},{2,1},{3,2},{4,7},{5,4},{6,5},{7,6},{8,11},{9,8},{10,9... | collective-permute-start | bytes 393224 | tf_op jit(solution)/shard_map/ppermute | solution.py:317
  29.5 0.9 copy-start.6
  84.1 34.5 %copy-start.12 = (f32[16,8]{0,1:T(8,128)S(1)}, f32[16,8]{0,1:T(8,128)}, u32[]{:S(2)}) copy-start(f32[16,8]{0,1:T(8,128)} %param.26) | copy-start | bytes 1540

commit v2 on v1

v2 whole, which is shorter than its diff:
```python
import jax
import jax.numpy as jnp
from jax import lax
from jax.experimental import pallas as pl
from jax.experimental.pallas import tpu as pltpu
from jax.sharding import PartitionSpec as P

LANES = 128
F32 = jnp.float32
BF16 = jnp.bfloat16
MIB = 1 << 20

GAP = 1

VMEM = pltpu.VMEM
SMEM = pltpu.SMEM


def whole(space=VMEM):
    return pl.BlockSpec(memory_space=space)


PROJ_STEPS = 4
CACHE_STEPS = 4


def attend_kernel(
    sec_ref,
    len_ref,
    q_hbm,
    kc_hbm,
    vc_hbm,
    nk_hbm,
    nv_hbm,
    wo_hbm,
    theirs_ref,
    mine_ref,
    q_ref,
    kc_ref,
    vc_ref,
    nk_ref,
    nv_ref,
    wo_ref,
    attn_ref,
    small_sems,
    key_sems,
    value_sems,
    wo_sems,
):
    rows, head_width = q_ref.shape
    heads = head_width // LANES
    positions = kc_ref.shape[0] // rows
    group = 16
    scale = 1.0 / LANES**0.5
    half = rows // 2
    block = wo_ref.shape[2]
    cache_rows = kc_ref.shape[0] // CACHE_STEPS

    small = [
        pltpu.make_async_copy(source, target, small_sems.at[i])
        for i, (source, target) in enumerate(((q_hbm, q_ref), (nk_hbm, nk_ref), (nv_hbm, nv_ref)))
    ]
    part = [pl.ds(i * cache_rows, cache_rows) for i in range(CACHE_STEPS)]
    key_copies = [pltpu.make_async_copy(kc_hbm.at[at], kc_ref.at[at], key_sems.at[i]) for i, at in enumerate(part)]
    value_copies = [pltpu.make_async_copy(vc_hbm.at[at], vc_ref.at[at], value_sems.at[i]) for i, at in enumerate(part)]
    wo_copies = [
        pltpu.make_async_copy(wo_hbm.at[:, pl.ds(i * block, block)], wo_ref.at[i], wo_sems.at[i])
        for i in range(PROJ_STEPS)
    ]
    for copy in small:
        copy.start()
    for i in range(CACHE_STEPS):
        key_copies[i].start()
        value_copies[i].start()
    for copy in wo_copies:
        copy.start()

    r = lax.broadcasted_iota(jnp.int32, (rows, rows), 0)
    c = lax.broadcasted_iota(jnp.int32, (rows, rows), 1)
    lengths = jnp.sum(jnp.where(r == c, len_ref[...], 0).astype(F32), axis=1, keepdims=True)
    span = group * positions
    row_token = lax.broadcasted_iota(jnp.int32, (heads * group, span), 0) % group
    column = lax.broadcasted_iota(jnp.int32, (heads * group, span), 1)
    own_column = column - row_token * positions
    own_position = jnp.where(own_column >= 0, own_column, positions).astype(F32)
    for copy in small:
        copy.wait()
    per_step = rows // group // CACHE_STEPS
    for g in range(rows // group):
        if g % per_step == 0:
            key_copies[g // per_step].wait()
            value_copies[g // per_step].wait()
        at = pl.ds(g * group, group)
        q = jnp.concatenate([q_ref[at, pl.ds(h * LANES, LANES)] for h in range(heads)], axis=0)
        keys = kc_ref[pl.ds(g * span, span), :]
        score = lax.dot_general(q, keys, (((1,), (1,)), ((), ())), preferred_element_type=F32) * scale
        new_key = jnp.concatenate([nk_ref[at, :].astype(F32)] * heads, axis=0)
        own_score = jnp.sum(q.astype(F32) * new_key, axis=1, keepdims=True) * scale
        limit = jnp.concatenate([lengths[g * group : (g + 1) * group]] * heads, axis=0)
        score = jnp.where(own_position < limit, score, -jnp.inf)
        highest = jnp.maximum(jnp.max(score, axis=1, keepdims=True), own_score)
        raised = jnp.exp(score - highest)
        own_raised = jnp.exp(own_score - highest)
        inverse = 1.0 / (jnp.sum(raised, axis=1, keepdims=True) + own_raised)
        weight = (raised * inverse).astype(BF16)
        own_weight = (own_raised * inverse).astype(BF16).astype(F32)
        values = vc_ref[pl.ds(g * span, span), :]
        out = jnp.dot(weight, values, preferred_element_type=F32)
        out = out + own_weight * jnp.concatenate([nv_ref[at, :].astype(F32)] * heads, axis=0)
        out = out.astype(BF16)
        place = lax.rem(g * group + half * (1 - sec_ref[0]), rows)
        place = pl.multiple_of(place, group)
        for h in range(heads):
            attn_ref[pl.ds(place, group), pl.ds(h * LANES, LANES)] = out[h * group : (h + 1) * group]

    for i in range(PROJ_STEPS):
        wo_copies[i].wait()
        proj = jnp.dot(attn_ref[...], wo_ref[i], preferred_element_type=F32)
        at = pl.ds(i * block, block)
        theirs_ref[:, at] = proj[:half].astype(BF16)
        mine_ref[:, at] = proj[half:].astype(BF16)


def attend(sec, lengths, q, kc, vc, nk, nv, wo):
    rows, head_width = q.shape
    width = wo.shape[1]
    out = jax.ShapeDtypeStruct((rows // 2, width), BF16)
    far = [pltpu.with_memory_space_constraint(a, pltpu.HBM) for a in (q, kc, vc, nk, nv, wo)]
    return pl.pallas_call(
        attend_kernel,
        in_specs=[whole(SMEM), whole()] + [whole(pltpu.HBM)] * 6,
        out_specs=[whole(), whole()],
        out_shape=[out, out],
        scratch_shapes=[pltpu.VMEM(a.shape, BF16) for a in (q, kc, vc, nk, nv)]
        + [
            pltpu.VMEM((PROJ_STEPS, head_width, width // PROJ_STEPS), BF16),
            pltpu.VMEM((rows, head_width), BF16),
            pltpu.SemaphoreType.DMA((3,)),
            pltpu.SemaphoreType.DMA((CACHE_STEPS,)),
            pltpu.SemaphoreType.DMA((CACHE_STEPS,)),
            pltpu.SemaphoreType.DMA((PROJ_STEPS,)),
        ],
        compiler_params=pltpu.CompilerParams(vmem_limit_bytes=14 * MIB),
        name="attend",
    )(sec, lengths, *far)


def quarter_kernel(kv_ref, mine_ref, got_ref, *out_refs):
    count = len(out_refs)
    rows = mine_ref.shape[0] // count
    for step, out_ref in enumerate(out_refs):
        at = pl.ds(pl.multiple_of(lax.rem(kv_ref[0] + step, count) * rows, rows), rows)
        out_ref[...] = (mine_ref[at, :].astype(F32) + got_ref[at, :].astype(F32)).astype(BF16)


def quarter(kv, mine, got, count):
    rows, width = mine.shape
    out = jax.ShapeDtypeStruct((rows // count, width), BF16)
    return pl.pallas_call(
        quarter_kernel,
        in_specs=[whole(SMEM), whole(), whole()],
        out_specs=[whole()] * count,
        out_shape=[out] * count,
        compiler_params=pltpu.CompilerParams(vmem_limit_bytes=4 * MIB),
        name="quarter",
    )(kv, mine, got)


def route_kernel(ids_ref, slots_ref, *refs):
    part_refs, (residual_ref, gain_ref, stream_ref, out_ref, wide_ref) = refs[:-5], refs[-5:]
    rows, width = residual_ref.shape
    pieces = width // LANES
    top = ids_ref.shape[0]
    stride = pieces + GAP
    out_ref[...] = jnp.zeros_like(out_ref)
    proj = part_refs[0][...].astype(F32)
    for part_ref in part_refs[1:]:
        proj = proj + part_ref[...].astype(F32)
    stream = (residual_ref[...].astype(F32) + proj).astype(BF16)
    stream_ref[...] = stream
    widened = stream.astype(F32)
    mean_square = jnp.mean(widened * widened, axis=-1, keepdims=True)
    normed = widened * lax.rsqrt(mean_square + 1e-06) * gain_ref[...]
    for t in range(0, rows, 8):
        for s in range(pieces):
            wide_ref[pl.ds(t * stride + s, 8, stride=stride), :] = normed[t : t + 8, s * LANES : (s + 1) * LANES]

    def one(t, carry):
        row = wide_ref[pl.ds(t * stride, pieces), :].astype(BF16)
        for k in range(top):
            out_ref[ids_ref[k, t], slots_ref[k, t]] = row
        return carry

    lax.fori_loop(0, rows, one, 0)


def route(ids, slots, parts, residual, gain, expert_count, capacity):
    rows, width = residual.shape
    pieces = width // LANES
    return pl.pallas_call(
        route_kernel,
        in_specs=[whole(SMEM), whole(SMEM)] + [whole()] * (len(parts) + 2),
        out_specs=[whole(), whole()],
        out_shape=[
            jax.ShapeDtypeStruct((rows, width), BF16),
            jax.ShapeDtypeStruct((expert_count, capacity, pieces, LANES), BF16),
        ],
        scratch_shapes=[pltpu.VMEM((rows * (pieces + GAP), LANES), F32)],
        compiler_params=pltpu.CompilerParams(vmem_limit_bytes=4 * MIB),
        name="route",
    )(ids, slots, *parts, residual, gain)


def load_kernel(*refs):
    count = len(refs) // 2
    sems = refs[-1]
    copies = [pltpu.make_async_copy(refs[i], refs[count + i], sems.at[i]) for i in range(count)]
    for copy in copies:
        copy.start()
    for copy in copies:
        copy.wait()


def load(*weights):
    size = sum(w.size * 2 for w in weights)
    return pl.pallas_call(
        load_kernel,
        in_specs=[whole(pltpu.HBM)] * len(weights),
        out_specs=[whole()] * len(weights),
        out_shape=[pltpu.VMEM(w.shape, w.dtype) for w in weights],
        scratch_shapes=[pltpu.SemaphoreType.DMA((len(weights),))],
        compiler_params=pltpu.CompilerParams(vmem_limit_bytes=2 * MIB),
        cost_estimate=pl.CostEstimate(flops=0, bytes_accessed=2 * size, transcendentals=0),
        name="load",
    )(*[pltpu.with_memory_space_constraint(w, pltpu.HBM) for w in weights])


def expert_kernel(x_ref, wg_ref, wu_ref, wd_ref, out_ref, wide_ref, flat_ref, hidden_ref):
    rows, pieces, _ = x_ref.shape
    hidden_width = wg_ref.shape[1]
    width = pieces * LANES
    stride = pieces + GAP
    ncols = 256
    dcols = 1024
    group = 16

    def spread(i, carry):
        base = pl.multiple_of(i * group, group)
        for r in range(group):
            wide_ref[pl.ds(r * stride, pieces), :] = x_ref[base + r].astype(F32)
        for s in range(pieces):
            low = wide_ref[pl.ds(s, 8, stride=stride), :]
            high = wide_ref[pl.ds(8 * stride + s, 8, stride=stride), :]
            flat_ref[pl.ds(base, group), pl.ds(s * LANES, LANES)] = jnp.concatenate([low, high], axis=0).astype(BF16)
        return carry

    lax.fori_loop(0, rows // group, spread, 0)

    for n in range(hidden_width // ncols):
        at = pl.ds(n * ncols, ncols)
        gate = jnp.dot(flat_ref[...], wg_ref[:, at], preferred_element_type=F32)
        up = jnp.dot(flat_ref[...], wu_ref[:, at], preferred_element_type=F32)
        hidden_ref[:, at] = (gate / (1.0 + jnp.exp(-gate)) * up).astype(BF16)

    for n in range(width // dcols):
        done = jnp.dot(hidden_ref[...], wd_ref[:, pl.ds(n * dcols, dcols)], preferred_element_type=F32)
        for r in range(0, rows, 8):
            for s in range(dcols // LANES):
                wide_ref[pl.ds(r * stride + n * (dcols // LANES) + s, 8, stride=stride), :] = done[
                    r : r + 8, s * LANES : (s + 1) * LANES
                ]

    def narrow(i, carry):
        base = pl.multiple_of(i * group, group)
        for r in range(group):
            out_ref[base + r] = wide_ref[pl.ds((base + r) * stride, pieces), :].astype(BF16)
        return carry

    lax.fori_loop(0, rows // group, narrow, 0)


def expert(x, wg, wu, wd):
    rows, pieces, _ = x.shape
    width, hidden_width = wg.shape
    near = [pltpu.with_memory_space_constraint(w, pltpu.VMEM) for w in (wg, wu, wd)]
    return pl.pallas_call(
        expert_kernel,
        in_specs=[whole()] * 4,
        out_specs=whole(),
        out_shape=jax.ShapeDtypeStruct(x.shape, BF16),
        scratch_shapes=[
            pltpu.VMEM((rows * (pieces + GAP), LANES), F32),
            pltpu.VMEM((rows, width), BF16),
            pltpu.VMEM((rows, hidden_width), BF16),
        ],
        compiler_params=pltpu.CompilerParams(vmem_limit_bytes=16 * MIB),
        name="expert",
    )(x, *near)


def combine_kernel(ids_ref, slots_ref, probs_ref, rows_ref, out_ref, wide_ref):
    rows, width = out_ref.shape
    pieces = width // LANES
    top = ids_ref.shape[0]
    stride = pieces + GAP

    def one(t, carry):
        total = None
        for k in range(top):
            term = rows_ref[ids_ref[k, t], slots_ref[k, t]].astype(F32) * probs_ref[k, t]
            total = term if total is None else total + term
        wide_ref[pl.ds(t * stride, pieces), :] = total
        return carry

    lax.fori_loop(0, rows, one, 0)
    for s in range(pieces):
        low = wide_ref[pl.ds(s, 8, stride=stride), :]
        high = wide_ref[pl.ds(8 * stride + s, 8, stride=stride), :]
        out_ref[:, pl.ds(s * LANES, LANES)] = jnp.concatenate([low, high], axis=0).astype(BF16)


def combine(ids, slots, probs, returned, width):
    rows = ids.shape[1]
    return pl.pallas_call(
        combine_kernel,
        in_specs=[whole(SMEM)] * 3 + [whole()],
        out_specs=whole(),
        out_shape=jax.ShapeDtypeStruct((rows, width), BF16),
        scratch_shapes=[pltpu.VMEM((rows * (width // LANES + GAP), LANES), F32)],
        compiler_params=pltpu.CompilerParams(vmem_limit_bytes=4 * MIB),
        name="combine",
    )(ids, slots, probs, returned)


def on_device(
    queries,
    key_cache,
    value_cache,
    new_keys,
    new_values,
    lengths,
    out_proj,
    residual,
    norm_gain,
    expert_ids,
    expert_slots,
    gate_probs,
    w_gate,
    w_up,
    w_down,
):
    row_count = queries.shape[0]
    width = out_proj.shape[1]
    pieces = width // LANES
    sec_count, group_count = lax.axis_size("sec"), lax.axis_size("kv")
    expert_count = sec_count * lax.axis_size("req") * group_count
    row_share, top_count = expert_ids.shape
    capacity = top_count * row_share // expert_count + 1
    sec = lax.axis_index("sec").astype(jnp.int32).reshape(1)
    kv = lax.axis_index("kv").astype(jnp.int32).reshape(1)

    theirs, mine = attend(
        sec,
        lengths.reshape(1, row_count),
        queries,
        key_cache.reshape(-1, LANES),
        value_cache.reshape(-1, LANES),
        new_keys.reshape(row_count, LANES),
        new_values.reshape(row_count, LANES),
        out_proj,
    )
    got = lax.ppermute(theirs, "sec", [(i, 1 - i) for i in range(sec_count)])
    quarters = quarter(kv, mine, got, group_count)
    parts = [quarters[0]] + [
        lax.ppermute(quarters[s], "kv", [(i, (i + s) % group_count) for i in range(group_count)])
        for s in range(1, group_count)
    ]
    ids, slots, probs = expert_ids.T, expert_slots.T, gate_probs.T
    stream, outgoing = route(ids, slots, parts, residual, norm_gain.reshape(1, width), expert_count, capacity)

    def exchange(rows):
        sent = rows.reshape(expert_count, capacity * pieces, LANES)
        return lax.all_to_all(sent, ("sec", "req", "kv"), split_axis=0, concat_axis=0, tiled=True)

    outgoing, *weights = lax.optimization_barrier((outgoing, *load(w_gate[0], w_up[0], w_down[0])))
    arrived = exchange(outgoing).reshape(expert_count * capacity, pieces, LANES)
    finished = expert(arrived, *weights)
    returned = exchange(finished).reshape(expert_count, capacity, pieces, LANES)
    moe_out = combine(ids, slots, probs, returned, width)
    return (stream, moe_out)


def solution(mesh):
    return jax.shard_map(
        on_device,
        mesh=mesh,
        in_specs=(
            P("req", ("kv", "sec")),
            P("req", "kv", None, None),
            P("req", "kv", None, None),
            P("req", "kv", None),
            P("req", "kv", None),
            P("req"),
            P(("kv", "sec"), None),
            P(("req", "sec", "kv"), None),
            P(),
            P(("req", "sec", "kv"), None),
            P(("req", "sec", "kv"), None),
            P(("req", "sec", "kv"), None),
            P(("sec", "req", "kv"), None, None),
            P(("sec", "req", "kv"), None, None),
            P(("sec", "req", "kv"), None, None),
        ),
        out_specs=(P(("req", "sec", "kv"), None), P(("req", "sec", "kv"), None)),
        check_vma=False,
    )
```

time: 121 us -> 105 us (0.87)
  local copies, waits for them, and re-layouts: 10.2 us -> 0.67 us
  waiting for transfers between devices: 6.64 us -> 1.54 us
  blocking collectives: 73.7 us -> 72.1 us
    unnamed x30 -> x12, local copies, waits for them, and re-layouts: 10.2 us -> 0.67 us
    ppermute x3, waiting for transfers between devices: 5.1 us -> 0.01 us  [on_device(): lax.ppermute(quarters[s], 'kv', [(i, (i + s) % group_count) for i in rang...]
    pallas_call x2 -> x3, Pallas kernels: 16.5 us -> 19.4 us  [the longest x1 6.95 us: attend(): pl.pallas_call(attend_kernel, in_specs=[whole(SMEM), whole()] + [whole(pl...]
    pallas_call x1, Pallas kernels: 2.02 us -> 0.12 us  [quarter(): pl.pallas_call(quarter_kernel, in_specs=[whole(SMEM), whole(), whole()],...]
    all_to_all x2, blocking collectives: 73.7 us -> 72.1 us  [exchange(): lax.all_to_all(sent, ('sec', 'req', 'kv'), split_axis=0, concat_axis=0, t...]
  transfers between devices with their start and end apart: 4 -> 4, of which waited for: 3 -> 1; matrix products, arithmetic and copies ran while one was open for 0% -> 0% of each run, Pallas kernels for 0% -> 6%
where the time goes in v2:
time: 105 us
  blocking collectives  72.1 us (69%)
  Pallas kernels  23.5 us (22%)
  starting transfers between devices  6.47 us (6%)
  waiting for transfers between devices  1.54 us (1%)
    all_to_all x2, blocking collectives, exchange(): lax.all_to_all(sent, ('sec', 'req', 'kv'), split_axis=0, concat_axis=0, t...  72.1 us
    pallas_call x1, Pallas kernels, attend(): pl.pallas_call(attend_kernel, in_specs=[whole(SMEM), whole()] + [whole(pl...  6.95 us
    pallas_call x1, Pallas kernels, load(): pl.pallas_call(load_kernel, in_specs=[whole(pltpu.HBM)] * len(weights), o...  6.45 us
    pallas_call x1, Pallas kernels, expert(): pl.pallas_call(expert_kernel, in_specs=[whole()] * 4, out_specs=whole(),...  5.96 us
    ppermute x3, starting transfers between devices, on_device(): lax.ppermute(quarters[s], 'kv', [(i, (i + s) % group_count) for i in rang...  4.96 us
    pallas_call x1, Pallas kernels, route(): pl.pallas_call(route_kernel, in_specs=[whole(SMEM), whole(SMEM)] + [whole...  2.19 us
  transfers between devices with their start and end apart: 4, of which 1 were waited for; matrix products, arithmetic and copies ran while one was open for 0% of the time, Pallas kernels for 6%

profile of v2, /device:TPU:1, one launch (start us, length us, event | category | flops | bytes accessed | tf_op | source)
XLA Modules:
  0.0 105.0 jit_solution(8963961274758461100)
XLA Ops:
  0.6 0.0 copy-start.5
  0.6 0.6 copy-done.5
  1.3 7.0 %attend.1 = (bf16[64,4096]{1,0:T(8,128)(2,1)S(1)}, bf16[64,4096]{1,0:T(8,128)(2,1)S(1)}) custom-call(s32[1]{0:T(128)} %bitcast.3.sec_ref, s32[1,128]{1,0:T(1,128)S(1)} %bitcast.28, bf16[128,512]{1,0:T(8,128)(2,1)} %q_hbm.1, bf16[4096,128]{1,0:T(8,128)(2,1)} %bitcast.32, bf16[4096,128]{1,0:T(8,128)(2,1)} %bitcast.33, bf16[128,128]{1,0:T(8,128)(2,1)} %bitcast.34, ...), custom_call_target="tpu_custom_call" | custom-call | tf_op jit(solution)/shard_map/attend/pallas_call | solution.py:129
  8.3 1.5 %collective-permute-start = (bf16[64,4096]{1,0:T(8,128)(2,1)S(1)}, bf16[64,4096]{1,0:T(8,128)(2,1)S(1)}, u32[]{:S(2)}, u32[]{:S(2)}) collective-permute-start(bf16[64,4096]{1,0:T(8,128)(2,1)S(1)} %get-tuple-element.18), channel_id=1, source_target_pairs={{0,64},{64,0},{1,65},{65,1},{2,66},{66,2},{3,67},{67,3},{4,68},{68... | collective-permute-start | bytes 1572872 | tf_op jit(solution)/shard_map/ppermute | solution.py:372
  9.8 1.5 %collective-permute-done.got_ref = bf16[64,4096]{1,0:T(8,128)(2,1)S(1)} collective-permute-done((bf16[64,4096]{1,0:T(8,128)(2,1)S(1)}, bf16[64,4096]{1,0:T(8,128)(2,1)S(1)}, u32[]{:S(2)}, u32[]{:S(2)}) %collective-permute-start) | collective-permute-done | bytes 524320 | tf_op jit(solution)/shard_map/ppermute | solution.py:372
  11.3 0.1 quarter.1
  11.4 1.4 %collective-permute-start.1 = (bf16[16,4096]{1,0:T(8,128)(2,1)S(1)}, bf16[16,4096]{1,0:T(8,128)(2,1)S(1)}, u32[]{:S(2)}, u32[]{:S(2)}) collective-permute-start(bf16[16,4096]{1,0:T(8,128)(2,1)S(1)} %get-tuple-element.20), channel_id=1, source_target_pairs={{0,1},{1,2},{2,3},{3,0},{4,5},{5,6},{6,7},{7,4},{8,9},{9,10},{10,1... | collective-permute-start | bytes 393224 | tf_op jit(solution)/shard_map/ppermute | solution.py:375
  12.8 2.4 %collective-permute-start.2 = (bf16[16,4096]{1,0:T(8,128)(2,1)S(1)}, bf16[16,4096]{1,0:T(8,128)(2,1)S(1)}, u32[]{:S(2)}, u32[]{:S(2)}) collective-permute-start(bf16[16,4096]{1,0:T(8,128)(2,1)S(1)} %get-tuple-element.21), channel_id=1, source_target_pairs={{0,2},{1,3},{2,0},{3,1},{4,6},{5,7},{6,4},{7,5},{8,10},{9,11},{10,... | collective-permute-start | bytes 393224 | tf_op jit(solution)/shard_map/ppermute | solution.py:375
  15.2 1.2 %collective-permute-start.3 = (bf16[16,4096]{1,0:T(8,128)(2,1)S(1)}, bf16[16,4096]{1,0:T(8,128)(2,1)S(1)}, u32[]{:S(2)}, u32[]{:S(2)}) collective-permute-start(bf16[16,4096]{1,0:T(8,128)(2,1)S(1)} %get-tuple-element.22), channel_id=1, source_target_pairs={{0,3},{1,0},{2,1},{3,2},{4,7},{5,4},{6,5},{7,6},{8,11},{9,8},{10,9... | collective-permute-start | bytes 393224 | tf_op jit(solution)/shard_map/ppermute | solution.py:375
  16.4 0.0 copy-start
  16.4 0.0 copy-start.1
  16.4 0.0 copy-start.2
  16.4 0.0 copy-start.3
  16.4 6.5 %load.1 = (bf16[4096,768]{1,0:T(8,128)(2,1)S(1)}, bf16[4096,768]{1,0:T(8,128)(2,1)S(1)}, bf16[768,4096]{1,0:T(8,128)(2,1)S(1)}) custom-call(bf16[4096,768]{1,0:T(8,128)(2,1)} %bitcast.29, bf16[4096,768]{1,0:T(8,128)(2,1)} %bitcast.30, bf16[768,4096]{1,0:T(8,128)(2,1)} %bitcast.31), custom_call_target="tpu_custom_call" | custom-call | bytes 37748736 | tf_op jit(solution)/shard_map/load/pallas_call | solution.py:226
  22.9 0.0 collective-permute-done.1.refs_1_
  22.9 0.0 collective-permute-done.2.refs_2_
  22.9 0.0 collective-permute-done.3.refs_3_
  22.9 0.0 copy-done
  22.9 0.0 copy-done.1
  22.9 0.0 copy-done.2
  22.9 0.0 copy-done.3
  22.9 2.2 %route.1 = (bf16[16,4096]{1,0:T(8,128)(2,1)}, bf16[128,2,32,128]{3,2,1,0:T(8,128)(2,1)S(1)}) custom-call(s32[8,16]{1,0:T(8,128)S(1)} %bitcast.22, s32[8,16]{1,0:T(8,128)S(1)} %bitcast.24, bf16[16,4096]{1,0:T(8,128)(2,1)S(1)} %get-tuple-element.19.refs_0_, bf16[16,4096]{1,0:T(8,128)(2,1)S(1)} %collective-permute-done.1.refs_1_, ...), custom_call_target="tpu_custom_call" | custom-call | tf_op jit(solution)/shard_map/route/pallas_call | solution.py:200
  25.1 37.6 %all_to_all.10 = bf16[128,64,128]{2,1,0:T(8,128)(2,1)S(1)} all-to-all(bf16[128,64,128]{2,1,0:T(8,128)(2,1)S(1)} %bitcast.21), channel_id=1, replica_groups=mesh['sec'=2,'req'=16,'kv'=4] {'sec','req','kv'}, dimensions={0} | all-to-all | bytes 4194304 | tf_op jit(solution)/shard_map/all_to_all | solution.py:383
  62.7 0.0 copy-start.4
  62.7 6.0 %expert.1 = bf16[256,32,128]{2,1,0:T(8,128)(2,1)S(1)} custom-call(bf16[256,32,128]{2,1,0:T(8,128)(2,1)S(1)} %bitcast.19, bf16[4096,768]{1,0:T(8,128)(2,1)S(1)} %get-tuple-element.29.wg_ref, bf16[4096,768]{1,0:T(8,128)(2,1)S(1)} %get-tuple-element.30.wu_ref, bf16[768,4096]{1,0:T(8,128)(2,1)S(1)} %get-tuple-element.31.wd_ref), custom_call_target="tpu_custom_call" | custom-call | tf_op jit(solution)/shard_map/expert/pallas_call | solution.py:286
  68.7 34.5 %all_to_all.11 = bf16[128,64,128]{2,1,0:T(8,128)(2,1)S(1)} all-to-all(bf16[128,64,128]{2,1,0:T(8,128)(2,1)S(1)} %bitcast.20), channel_id=1, replica_groups=mesh['sec'=2,'req'=16,'kv'=4] {'sec','req','kv'}, dimensions={0} | all-to-all | bytes 4194304 | tf_op jit(solution)/shard_map/all_to_all | solution.py:383
  103.2 0.0 copy-done.4
  103.2 1.9 %combine.1 = bf16[16,4096]{1,0:T(8,128)(2,1)} custom-call(s32[8,16]{1,0:T(8,128)S(1)} %bitcast.23, s32[8,16]{1,0:T(8,128)S(1)} %bitcast.25, f32[8,16]{1,0:T(8,128)S(1)} %bitcast.27, bf16[128,2,32,128]{3,2,1,0:T(8,128)(2,1)S(1)} %bitcast.18), custom_call_target="tpu_custom_call" | custom-call | tf_op jit(solution)/shard_map/combine/pallas_call | solution.py:324
Async XLA Ops:
  0.6 0.7 copy-start.5
  8.3 3.0 %collective-permute-start = (bf16[64,4096]{1,0:T(8,128)(2,1)S(1)}, bf16[64,4096]{1,0:T(8,128)(2,1)S(1)}, u32[]{:S(2)}, u32[]{:S(2)}) collective-permute-start(bf16[64,4096]{1,0:T(8,128)(2,1)S(1)} %get-tuple-element.18), channel_id=1, source_target_pairs={{0,64},{64,0},{1,65},{65,1},{2,66},{66,2},{3,67},{67,3},{4,68},{68... | collective-permute-start | bytes 1572872 | tf_op jit(solution)/shard_map/ppermute | solution.py:372
  11.4 11.4 %collective-permute-start.1 = (bf16[16,4096]{1,0:T(8,128)(2,1)S(1)}, bf16[16,4096]{1,0:T(8,128)(2,1)S(1)}, u32[]{:S(2)}, u32[]{:S(2)}) collective-permute-start(bf16[16,4096]{1,0:T(8,128)(2,1)S(1)} %get-tuple-element.20), channel_id=1, source_target_pairs={{0,1},{1,2},{2,3},{3,0},{4,5},{5,6},{6,7},{7,4},{8,9},{9,10},{10,1... | collective-permute-start | bytes 393224 | tf_op jit(solution)/shard_map/ppermute | solution.py:375
  12.8 10.1 %collective-permute-start.2 = (bf16[16,4096]{1,0:T(8,128)(2,1)S(1)}, bf16[16,4096]{1,0:T(8,128)(2,1)S(1)}, u32[]{:S(2)}, u32[]{:S(2)}) collective-permute-start(bf16[16,4096]{1,0:T(8,128)(2,1)S(1)} %get-tuple-element.21), channel_id=1, source_target_pairs={{0,2},{1,3},{2,0},{3,1},{4,6},{5,7},{6,4},{7,5},{8,10},{9,11},{10,... | collective-permute-start | bytes 393224 | tf_op jit(solution)/shard_map/ppermute | solution.py:375
  15.2 7.7 %collective-permute-start.3 = (bf16[16,4096]{1,0:T(8,128)(2,1)S(1)}, bf16[16,4096]{1,0:T(8,128)(2,1)S(1)}, u32[]{:S(2)}, u32[]{:S(2)}) collective-permute-start(bf16[16,4096]{1,0:T(8,128)(2,1)S(1)} %get-tuple-element.22), channel_id=1, source_target_pairs={{0,3},{1,0},{2,1},{3,2},{4,7},{5,4},{6,5},{7,6},{8,11},{9,8},{10,9... | collective-permute-start | bytes 393224 | tf_op jit(solution)/shard_map/ppermute | solution.py:375
  16.4 6.5 %copy-start = (bf16[16,4096]{1,0:T(8,128)(2,1)S(1)}, bf16[16,4096]{1,0:T(8,128)(2,1)}, u32[]{:S(2)}) copy-start(bf16[16,4096]{1,0:T(8,128)(2,1)} %refs_4_.1) | copy-start | bytes 393220
  16.4 6.5 %copy-start.1 = (s32[16,8]{0,1:T(8,128)S(1)}, s32[16,8]{0,1:T(8,128)}, u32[]{:S(2)}) copy-start(s32[16,8]{0,1:T(8,128)} %param.24) | copy-start | bytes 1540
  16.4 6.5 %copy-start.2 = (s32[16,8]{0,1:T(8,128)S(1)}, s32[16,8]{0,1:T(8,128)}, u32[]{:S(2)}) copy-start(s32[16,8]{0,1:T(8,128)} %param.25) | copy-start | bytes 1540
  16.4 6.5 %copy-start.3 = (f32[4096]{0:T(1024)S(1)}, f32[4096]{0:T(1024)}, u32[]{:S(2)}) copy-start(f32[4096]{0:T(1024)} %param.23) | copy-start | bytes 49156
  62.7 40.4 %copy-start.4 = (f32[16,8]{0,1:T(8,128)S(1)}, f32[16,8]{0,1:T(8,128)}, u32[]{:S(2)}) copy-start(f32[16,8]{0,1:T(8,128)} %param.26) | copy-start | bytes 1540

commit v3 on v2

--- a/solution.py
+++ b/solution.py
@@ -1,3 +1,5 @@
+import math
+
 import jax
 import jax.numpy as jnp
 from jax import lax
@@ -20,13 +22,9 @@
     return pl.BlockSpec(memory_space=space)
 
 
-PROJ_STEPS = 4
-CACHE_STEPS = 4
-
-
 def attend_kernel(
     sec_ref,
-    len_ref,
+    len_hbm,
     q_hbm,
     kc_hbm,
     vc_hbm,
@@ -35,6 +33,7 @@
     wo_hbm,
     theirs_ref,
     mine_ref,
+    len_ref,
     q_ref,
     kc_ref,
     vc_ref,
@@ -42,39 +41,27 @@
     nv_ref,
     wo_ref,
     attn_ref,
-    small_sems,
-    key_sems,
-    value_sems,
-    wo_sems,
+    sems,
 ):
     rows, head_width = q_ref.shape
     heads = head_width // LANES
     positions = kc_ref.shape[0] // rows
-    group = 16
-    scale = 1.0 / LANES**0.5
+    group = 8
+    to_exponent = math.log2(math.e) / LANES**0.5
     half = rows // 2
-    block = wo_ref.shape[2]
-    cache_rows = kc_ref.shape[0] // CACHE_STEPS
 
     small = [
-        pltpu.make_async_copy(source, target, small_sems.at[i])
-        for i, (source, target) in enumerate(((q_hbm, q_ref), (nk_hbm, nk_ref), (nv_hbm, nv_ref)))
+        pltpu.make_async_copy(source, target, sems.at[i])
+        for i, (source, target) in enumerate(((len_hbm, len_ref), (q_hbm, q_ref), (nk_hbm, nk_ref), (nv_hbm, nv_ref)))
     ]
-    part = [pl.ds(i * cache_rows, cache_rows) for i in range(CACHE_STEPS)]
-    key_copies = [pltpu.make_async_copy(kc_hbm.at[at], kc_ref.at[at], key_sems.at[i]) for i, at in enumerate(part)]
-    value_copies = [pltpu.make_async_copy(vc_hbm.at[at], vc_ref.at[at], value_sems.at[i]) for i, at in enumerate(part)]
-    wo_copies = [
-        pltpu.make_async_copy(wo_hbm.at[:, pl.ds(i * block, block)], wo_ref.at[i], wo_sems.at[i])
-        for i in range(PROJ_STEPS)
-    ]
+    key_copy = pltpu.make_async_copy(kc_hbm, kc_ref, sems.at[4])
+    value_copy = pltpu.make_async_copy(vc_hbm, vc_ref, sems.at[5])
+    wo_copy = pltpu.make_async_copy(wo_hbm, wo_ref, sems.at[6])
+    for copy in (*small, key_copy, value_copy, wo_copy):
+        copy.start()
+
     for copy in small:
-        copy.start()
-    for i in range(CACHE_STEPS):
-        key_copies[i].start()
-        value_copies[i].start()
-    for copy in wo_copies:
-        copy.start()
-
+        copy.wait()
     r = lax.broadcasted_iota(jnp.int32, (rows, rows), 0)
     c = lax.broadcasted_iota(jnp.int32, (rows, rows), 1)
     lengths = jnp.sum(jnp.where(r == c, len_ref[...], 0).astype(F32), axis=1, keepdims=True)
@@ -83,66 +70,66 @@
     column = lax.broadcasted_iota(jnp.int32, (heads * group, span), 1)
     own_column = column - row_token * positions
     own_position = jnp.where(own_column >= 0, own_column, positions).astype(F32)
-    for copy in small:
-        copy.wait()
-    per_step = rows // group // CACHE_STEPS
-    for g in range(rows // group):
-        if g % per_step == 0:
-            key_copies[g // per_step].wait()
-            value_copies[g // per_step].wait()
-        at = pl.ds(g * group, group)
-        q = jnp.concatenate([q_ref[at, pl.ds(h * LANES, LANES)] for h in range(heads)], axis=0)
+
+    def per_head(rows_of_group):
+        return jnp.concatenate([rows_of_group] * heads, axis=0)
+
+    def group_rows(ref, g):
+        pair = ref[pl.ds(g // 2 * 2 * group, 2 * group), :].astype(F32)
+        return pair[g % 2 * group : (g % 2 + 1) * group]
+
+    groups = rows // group
+    scores, own_scores, raised, own_raised, outs = [], [], [], [], []
+    key_copy.wait()
+    for g in range(groups):
+        q_rows = group_rows(q_ref, g)
+        q = jnp.concatenate([q_rows[:, h * LANES : (h + 1) * LANES] for h in range(heads)], axis=0)
         keys = kc_ref[pl.ds(g * span, span), :]
-        score = lax.dot_general(q, keys, (((1,), (1,)), ((), ())), preferred_element_type=F32) * scale
-        new_key = jnp.concatenate([nk_ref[at, :].astype(F32)] * heads, axis=0)
-        own_score = jnp.sum(q.astype(F32) * new_key, axis=1, keepdims=True) * scale
-        limit = jnp.concatenate([lengths[g * group : (g + 1) * group]] * heads, axis=0)
-        score = jnp.where(own_position < limit, score, -jnp.inf)
+        score = lax.dot_general(q.astype(BF16), keys, (((1,), (1,)), ((), ())), preferred_element_type=F32)
+        scores.append(jnp.where(own_position < per_head(lengths[g * group : (g + 1) * group]), score, -jnp.inf))
+        own_scores.append(jnp.sum(q * per_head(group_rows(nk_ref, g)), axis=1, keepdims=True))
+    for score, own_score in zip(scores, own_scores):
         highest = jnp.maximum(jnp.max(score, axis=1, keepdims=True), own_score)
-        raised = jnp.exp(score - highest)
-        own_raised = jnp.exp(own_score - highest)
-        inverse = 1.0 / (jnp.sum(raised, axis=1, keepdims=True) + own_raised)
-        weight = (raised * inverse).astype(BF16)
-        own_weight = (own_raised * inverse).astype(BF16).astype(F32)
+        raised.append(jnp.exp2((score - highest) * to_exponent))
+        own_raised.append(jnp.exp2((own_score - highest) * to_exponent))
+    value_copy.wait()
+    for g in range(groups):
+        inverse = 1.0 / (jnp.sum(raised[g], axis=1, keepdims=True) + own_raised[g])
         values = vc_ref[pl.ds(g * span, span), :]
-        out = jnp.dot(weight, values, preferred_element_type=F32)
-        out = out + own_weight * jnp.concatenate([nv_ref[at, :].astype(F32)] * heads, axis=0)
-        out = out.astype(BF16)
+        out = jnp.dot(raised[g].astype(BF16), values, preferred_element_type=F32)
+        outs.append((out + own_raised[g] * per_head(group_rows(nv_ref, g))) * inverse)
+    for g in range(0, groups, 2):
         place = lax.rem(g * group + half * (1 - sec_ref[0]), rows)
-        place = pl.multiple_of(place, group)
+        place = pl.multiple_of(place, 2 * group)
         for h in range(heads):
-            attn_ref[pl.ds(place, group), pl.ds(h * LANES, LANES)] = out[h * group : (h + 1) * group]
-
-    for i in range(PROJ_STEPS):
-        wo_copies[i].wait()
-        proj = jnp.dot(attn_ref[...], wo_ref[i], preferred_element_type=F32)
-        at = pl.ds(i * block, block)
-        theirs_ref[:, at] = proj[:half].astype(BF16)
-        mine_ref[:, at] = proj[half:].astype(BF16)
+            pair = [outs[g + j][h * group : (h + 1) * group] for j in range(2)]
+            attn_ref[pl.ds(place, 2 * group), pl.ds(h * LANES, LANES)] = jnp.concatenate(pair, axis=0).astype(BF16)
+
+    wo_copy.wait()
+    proj = jnp.dot(attn_ref[...], wo_ref[...], preferred_element_type=F32)
+    theirs_ref[...] = proj[:half].astype(BF16)
+    mine_ref[...] = proj[half:].astype(BF16)
 
 
 def attend(sec, lengths, q, kc, vc, nk, nv, wo):
     rows, head_width = q.shape
     width = wo.shape[1]
     out = jax.ShapeDtypeStruct((rows // 2, width), BF16)
-    far = [pltpu.with_memory_space_constraint(a, pltpu.HBM) for a in (q, kc, vc, nk, nv, wo)]
+    far = [pltpu.with_memory_space_constraint(a, pltpu.HBM) for a in (lengths, q, kc, vc, nk, nv, wo)]
     return pl.pallas_call(
         attend_kernel,
-        in_specs=[whole(SMEM), whole()] + [whole(pltpu.HBM)] * 6,
+        in_specs=[whole(SMEM)] + [whole(pltpu.HBM)] * 7,
         out_specs=[whole(), whole()],
         out_shape=[out, out],
-        scratch_shapes=[pltpu.VMEM(a.shape, BF16) for a in (q, kc, vc, nk, nv)]
+        scratch_shapes=[pltpu.VMEM(a.shape, a.dtype) for a in (lengths, q, kc, vc, nk, nv)]
         + [
-            pltpu.VMEM((PROJ_STEPS, head_width, width // PROJ_STEPS), BF16),
+            pltpu.VMEM(wo.shape, BF16),
             pltpu.VMEM((rows, head_width), BF16),
-            pltpu.SemaphoreType.DMA((3,)),
-            pltpu.SemaphoreType.DMA((CACHE_STEPS,)),
-            pltpu.SemaphoreType.DMA((CACHE_STEPS,)),
-            pltpu.SemaphoreType.DMA((PROJ_STEPS,)),
+            pltpu.SemaphoreType.DMA((7,)),
         ],
         compiler_params=pltpu.CompilerParams(vmem_limit_bytes=14 * MIB),
         name="attend",
-    )(sec, lengths, *far)
+    )(sec, *far)
 
 
 def quarter_kernel(kv_ref, mine_ref, got_ref, *out_refs):
@@ -167,7 +154,7 @@
 
 
 def route_kernel(ids_ref, slots_ref, *refs):
-    part_refs, (residual_ref, gain_ref, stream_ref, out_ref, wide_ref) = refs[:-5], refs[-5:]
+    part_refs, (residual_ref, gain_ref, stream_hbm, out_ref, wide_ref, stream_ref, sem) = refs[:-7], refs[-7:]
     rows, width = residual_ref.shape
     pieces = width // LANES
     top = ids_ref.shape[0]
@@ -178,6 +165,8 @@
         proj = proj + part_ref[...].astype(F32)
     stream = (residual_ref[...].astype(F32) + proj).astype(BF16)
     stream_ref[...] = stream
+    leave = pltpu.make_async_copy(stream_ref, stream_hbm, sem)
+    leave.start()
     widened = stream.astype(F32)
     mean_square = jnp.mean(widened * widened, axis=-1, keepdims=True)
     normed = widened * lax.rsqrt(mean_square + 1e-06) * gain_ref[...]
@@ -191,7 +180,8 @@
             out_ref[ids_ref[k, t], slots_ref[k, t]] = row
         return carry
 
-    lax.fori_loop(0, rows, one, 0)
+    lax.fori_loop(0, rows, one, 0, unroll=4)
+    leave.wait()
 
 
 def route(ids, slots, parts, residual, gain, expert_count, capacity):
@@ -200,12 +190,16 @@
     return pl.pallas_call(
         route_kernel,
         in_specs=[whole(SMEM), whole(SMEM)] + [whole()] * (len(parts) + 2),
-        out_specs=[whole(), whole()],
+        out_specs=[whole(pl.ANY), whole()],
         out_shape=[
             jax.ShapeDtypeStruct((rows, width), BF16),
             jax.ShapeDtypeStruct((expert_count, capacity, pieces, LANES), BF16),
         ],
-        scratch_shapes=[pltpu.VMEM((rows * (pieces + GAP), LANES), F32)],
+        scratch_shapes=[
+            pltpu.VMEM((rows * (pieces + GAP), LANES), F32),
+            pltpu.VMEM((rows, width), BF16),
+            pltpu.SemaphoreType.DMA,
+        ],
         compiler_params=pltpu.CompilerParams(vmem_limit_bytes=4 * MIB),
         name="route",
     )(ids, slots, *parts, residual, gain)
@@ -235,7 +229,7 @@
     )(*[pltpu.with_memory_space_constraint(w, pltpu.HBM) for w in weights])
 
 
-def expert_kernel(x_ref, wg_ref, wu_ref, wd_ref, out_ref, wide_ref, flat_ref, hidden_ref):
+def expert_kernel(x_ref, wg_ref, wu_ref, wd_hbm, out_ref, wide_ref, flat_ref, hidden_ref, wd_ref, sem):
     rows, pieces, _ = x_ref.shape
     hidden_width = wg_ref.shape[1]
     width = pieces * LANES
@@ -243,6 +237,8 @@
     ncols = 256
     dcols = 1024
     group = 16
+    down_copy = pltpu.make_async_copy(wd_hbm, wd_ref, sem)
+    down_copy.start()
 
     def spread(i, carry):
         base = pl.multiple_of(i * group, group)
@@ -262,6 +258,7 @@
         up = jnp.dot(flat_ref[...], wu_ref[:, at], preferred_element_type=F32)
         hidden_ref[:, at] = (gate / (1.0 + jnp.exp(-gate)) * up).astype(BF16)
 
+    down_copy.wait()
     for n in range(width // dcols):
         done = jnp.dot(hidden_ref[...], wd_ref[:, pl.ds(n * dcols, dcols)], preferred_element_type=F32)
         for r in range(0, rows, 8):
@@ -282,20 +279,22 @@
 def expert(x, wg, wu, wd):
     rows, pieces, _ = x.shape
     width, hidden_width = wg.shape
-    near = [pltpu.with_memory_space_constraint(w, pltpu.VMEM) for w in (wg, wu, wd)]
+    near = [pltpu.with_memory_space_constraint(w, pltpu.VMEM) for w in (wg, wu)]
     return pl.pallas_call(
         expert_kernel,
-        in_specs=[whole()] * 4,
+        in_specs=[whole()] * 3 + [whole(pltpu.HBM)],
         out_specs=whole(),
         out_shape=jax.ShapeDtypeStruct(x.shape, BF16),
         scratch_shapes=[
             pltpu.VMEM((rows * (pieces + GAP), LANES), F32),
             pltpu.VMEM((rows, width), BF16),
             pltpu.VMEM((rows, hidden_width), BF16),
+            pltpu.VMEM(wd.shape, BF16),
+            pltpu.SemaphoreType.DMA,
         ],
-        compiler_params=pltpu.CompilerParams(vmem_limit_bytes=16 * MIB),
+        compiler_params=pltpu.CompilerParams(vmem_limit_bytes=20 * MIB),
         name="expert",
-    )(x, *near)
+    )(x, *near, pltpu.with_memory_space_constraint(wd, pltpu.HBM))
 
 
 def combine_kernel(ids_ref, slots_ref, probs_ref, rows_ref, out_ref, wide_ref):
@@ -312,7 +311,7 @@
         wide_ref[pl.ds(t * stride, pieces), :] = total
         return carry
 
-    lax.fori_loop(0, rows, one, 0)
+    lax.fori_loop(0, rows, one, 0, unroll=4)
     for s in range(pieces):
         low = wide_ref[pl.ds(s, 8, stride=stride), :]
         high = wide_ref[pl.ds(8 * stride + s, 8, stride=stride), :]
@@ -382,9 +381,9 @@
         sent = rows.reshape(expert_count, capacity * pieces, LANES)
         return lax.all_to_all(sent, ("sec", "req", "kv"), split_axis=0, concat_axis=0, tiled=True)
 
-    outgoing, *weights = lax.optimization_barrier((outgoing, *load(w_gate[0], w_up[0], w_down[0])))
+    outgoing, *weights = lax.optimization_barrier((outgoing, *load(w_gate[0], w_up[0])))
     arrived = exchange(outgoing).reshape(expert_count * capacity, pieces, LANES)
-    finished = expert(arrived, *weights)
+    finished = expert(arrived, *weights, w_down[0])
     returned = exchange(finished).reshape(expert_count, capacity, pieces, LANES)
     moe_out = combine(ids, slots, probs, returned, width)
     return (stream, moe_out)

time: 105 us -> 101 us (0.962)
  Pallas kernels: 23.5 us -> 17.9 us
  blocking collectives: 72.1 us -> 73.7 us
    pallas_call x2, Pallas kernels: 12.9 us -> 9.89 us  [the longest x1 6.15 us: expert(): pl.pallas_call(expert_kernel, in_specs=[whole()] * 3 + [whole(pltpu.HBM)]...]
    pallas_call x1, Pallas kernels: 6.45 us -> 4.65 us  [load(): pl.pallas_call(load_kernel, in_specs=[whole(pltpu.HBM)] * len(weights), o...]
    all_to_all x2, blocking collectives: 72.1 us -> 73.7 us  [exchange(): lax.all_to_all(sent, ('sec', 'req', 'kv'), split_axis=0, concat_axis=0, t...]
  transfers between devices with their start and end apart: 4 -> 4, of which waited for: 1 -> 2; matrix products, arithmetic and copies ran while one was open for 0% -> 0% of each run, Pallas kernels for 6% -> 5%
where the time goes in v3:
time: 101 us
  blocking collectives  73.7 us (73%)
  Pallas kernels  17.9 us (18%)
  starting transfers between devices  6.47 us (6%)
  waiting for transfers between devices  1.76 us (2%)
    all_to_all x2, blocking collectives, exchange(): lax.all_to_all(sent, ('sec', 'req', 'kv'), split_axis=0, concat_axis=0, t...  73.7 us
    pallas_call x1, Pallas kernels, expert(): pl.pallas_call(expert_kernel, in_specs=[whole()] * 3 + [whole(pltpu.HBM)]...  6.15 us
    ppermute x3, starting transfers between devices, on_device(): lax.ppermute(quarters[s], 'kv', [(i, (i + s) % group_count) for i in rang...  4.96 us
    pallas_call x1, Pallas kernels, load(): pl.pallas_call(load_kernel, in_specs=[whole(pltpu.HBM)] * len(weights), o...  4.65 us
    pallas_call x1, Pallas kernels, attend(): pl.pallas_call(attend_kernel, in_specs=[whole(SMEM)] + [whole(pltpu.HBM)]...  3.74 us
  transfers between devices with their start and end apart: 4, of which 2 were waited for; matrix products, arithmetic and copies ran while one was open for 0% of the time, Pallas kernels for 5%

profile of v3, /device:TPU:1, one launch (start us, length us, event | category | flops | bytes accessed | tf_op | source)
XLA Modules:
  0.0 100.6 jit_solution(5872894042702654151)
XLA Ops:
  0.6 3.7 %attend.1 = (bf16[64,4096]{1,0:T(8,128)(2,1)S(1)}, bf16[64,4096]{1,0:T(8,128)(2,1)S(1)}) custom-call(s32[1]{0:T(128)} %bitcast.3.sec_ref, s32[1,128]{1,0:T(1,128)} %bitcast.35, bf16[128,512]{1,0:T(8,128)(2,1)} %q_hbm.1, bf16[4096,128]{1,0:T(8,128)(2,1)} %bitcast.31, bf16[4096,128]{1,0:T(8,128)(2,1)} %bitcast.32, bf16[128,128]{1,0:T(8,128)(2,1)} %bitcast.33, ...), custom_call_target="tpu_custom_call" | custom-call | tf_op jit(solution)/shard_map/attend/pallas_call | solution.py:119
  4.4 1.5 %collective-permute-start = (bf16[64,4096]{1,0:T(8,128)(2,1)S(1)}, bf16[64,4096]{1,0:T(8,128)(2,1)S(1)}, u32[]{:S(2)}, u32[]{:S(2)}) collective-permute-start(bf16[64,4096]{1,0:T(8,128)(2,1)S(1)} %get-tuple-element.16), channel_id=1, source_target_pairs={{0,64},{64,0},{1,65},{65,1},{2,66},{66,2},{3,67},{67,3},{4,68},{68... | collective-permute-start | bytes 1572872 | tf_op jit(solution)/shard_map/ppermute | solution.py:371
  5.9 1.5 %collective-permute-done.got_ref = bf16[64,4096]{1,0:T(8,128)(2,1)S(1)} collective-permute-done((bf16[64,4096]{1,0:T(8,128)(2,1)S(1)}, bf16[64,4096]{1,0:T(8,128)(2,1)S(1)}, u32[]{:S(2)}, u32[]{:S(2)}) %collective-permute-start) | collective-permute-done | bytes 524320 | tf_op jit(solution)/shard_map/ppermute | solution.py:371
  7.4 0.1 quarter.1
  7.6 1.4 %collective-permute-start.1 = (bf16[16,4096]{1,0:T(8,128)(2,1)S(1)}, bf16[16,4096]{1,0:T(8,128)(2,1)S(1)}, u32[]{:S(2)}, u32[]{:S(2)}) collective-permute-start(bf16[16,4096]{1,0:T(8,128)(2,1)S(1)} %get-tuple-element.18), channel_id=1, source_target_pairs={{0,1},{1,2},{2,3},{3,0},{4,5},{5,6},{6,7},{7,4},{8,9},{9,10},{10,1... | collective-permute-start | bytes 393224 | tf_op jit(solution)/shard_map/ppermute | solution.py:374
  8.9 2.4 %collective-permute-start.2 = (bf16[16,4096]{1,0:T(8,128)(2,1)S(1)}, bf16[16,4096]{1,0:T(8,128)(2,1)S(1)}, u32[]{:S(2)}, u32[]{:S(2)}) collective-permute-start(bf16[16,4096]{1,0:T(8,128)(2,1)S(1)} %get-tuple-element.19), channel_id=1, source_target_pairs={{0,2},{1,3},{2,0},{3,1},{4,6},{5,7},{6,4},{7,5},{8,10},{9,11},{10,... | collective-permute-start | bytes 393224 | tf_op jit(solution)/shard_map/ppermute | solution.py:374
  11.4 1.2 %collective-permute-start.3 = (bf16[16,4096]{1,0:T(8,128)(2,1)S(1)}, bf16[16,4096]{1,0:T(8,128)(2,1)S(1)}, u32[]{:S(2)}, u32[]{:S(2)}) collective-permute-start(bf16[16,4096]{1,0:T(8,128)(2,1)S(1)} %get-tuple-element.20), channel_id=1, source_target_pairs={{0,3},{1,0},{2,1},{3,2},{4,7},{5,4},{6,5},{7,6},{8,11},{9,8},{10,9... | collective-permute-start | bytes 393224 | tf_op jit(solution)/shard_map/ppermute | solution.py:374
  12.5 0.0 copy-start
  12.5 0.0 copy-start.1
  12.5 0.0 copy-start.2
  12.5 0.0 copy-start.3
  12.5 4.7 %load.1 = (bf16[4096,768]{1,0:T(8,128)(2,1)S(1)}, bf16[4096,768]{1,0:T(8,128)(2,1)S(1)}) custom-call(bf16[4096,768]{1,0:T(8,128)(2,1)} %bitcast.28, bf16[4096,768]{1,0:T(8,128)(2,1)} %bitcast.29), custom_call_target="tpu_custom_call" | custom-call | bytes 25165824 | tf_op jit(solution)/shard_map/load/pallas_call | solution.py:220
  17.2 0.0 collective-permute-done.1.refs_1_
  17.2 0.2 collective-permute-done.2.refs_2_
  17.4 0.0 collective-permute-done.3.refs_3_
  17.4 0.0 copy-done
  17.4 0.0 copy-done.1
  17.4 0.0 copy-done.2
  17.4 0.0 copy-done.3
  17.4 1.5 %route.1 = (bf16[16,4096]{1,0:T(8,128)(2,1)}, bf16[128,2,32,128]{3,2,1,0:T(8,128)(2,1)S(1)}) custom-call(s32[8,16]{1,0:T(8,128)S(1)} %bitcast.22, s32[8,16]{1,0:T(8,128)S(1)} %bitcast.24, bf16[16,4096]{1,0:T(8,128)(2,1)S(1)} %get-tuple-element.17.refs_0_, bf16[16,4096]{1,0:T(8,128)(2,1)S(1)} %collective-permute-done.1.refs_1_, ...), custom_call_target="tpu_custom_call" | custom-call | tf_op jit(solution)/shard_map/route/pallas_call | solution.py:190
  18.9 39.2 %all_to_all.10 = bf16[128,64,128]{2,1,0:T(8,128)(2,1)S(1)} all-to-all(bf16[128,64,128]{2,1,0:T(8,128)(2,1)S(1)} %bitcast.21), channel_id=1, replica_groups=mesh['sec'=2,'req'=16,'kv'=4] {'sec','req','kv'}, dimensions={0} | all-to-all | bytes 4194304 | tf_op jit(solution)/shard_map/all_to_all | solution.py:382
  58.1 0.0 copy-start.4
  58.1 6.1 %expert.1 = bf16[256,32,128]{2,1,0:T(8,128)(2,1)S(1)} custom-call(bf16[256,32,128]{2,1,0:T(8,128)(2,1)S(1)} %bitcast.19, bf16[4096,768]{1,0:T(8,128)(2,1)S(1)} %get-tuple-element.26.wg_ref, bf16[4096,768]{1,0:T(8,128)(2,1)S(1)} %get-tuple-element.27.wu_ref, bf16[768,4096]{1,0:T(8,128)(2,1)} %bitcast.30), custom_call_target="tpu_custom_call" | custom-call | tf_op jit(solution)/shard_map/expert/pallas_call | solution.py:283
  64.3 34.5 %all_to_all.11 = bf16[128,64,128]{2,1,0:T(8,128)(2,1)S(1)} all-to-all(bf16[128,64,128]{2,1,0:T(8,128)(2,1)S(1)} %bitcast.20), channel_id=1, replica_groups=mesh['sec'=2,'req'=16,'kv'=4] {'sec','req','kv'}, dimensions={0} | all-to-all | bytes 4194304 | tf_op jit(solution)/shard_map/all_to_all | solution.py:382
  98.8 0.0 copy-done.4
  98.8 1.8 %combine.1 = bf16[16,4096]{1,0:T(8,128)(2,1)} custom-call(s32[8,16]{1,0:T(8,128)S(1)} %bitcast.23, s32[8,16]{1,0:T(8,128)S(1)} %bitcast.25, f32[8,16]{1,0:T(8,128)S(1)} %bitcast.27, bf16[128,2,32,128]{3,2,1,0:T(8,128)(2,1)S(1)} %bitcast.18), custom_call_target="tpu_custom_call" | custom-call | tf_op jit(solution)/shard_map/combine/pallas_call | solution.py:323
Async XLA Ops:
  4.4 3.0 %collective-permute-start = (bf16[64,4096]{1,0:T(8,128)(2,1)S(1)}, bf16[64,4096]{1,0:T(8,128)(2,1)S(1)}, u32[]{:S(2)}, u32[]{:S(2)}) collective-permute-start(bf16[64,4096]{1,0:T(8,128)(2,1)S(1)} %get-tuple-element.16), channel_id=1, source_target_pairs={{0,64},{64,0},{1,65},{65,1},{2,66},{66,2},{3,67},{67,3},{4,68},{68... | collective-permute-start | bytes 1572872 | tf_op jit(solution)/shard_map/ppermute | solution.py:371
  7.6 9.6 %collective-permute-start.1 = (bf16[16,4096]{1,0:T(8,128)(2,1)S(1)}, bf16[16,4096]{1,0:T(8,128)(2,1)S(1)}, u32[]{:S(2)}, u32[]{:S(2)}) collective-permute-start(bf16[16,4096]{1,0:T(8,128)(2,1)S(1)} %get-tuple-element.18), channel_id=1, source_target_pairs={{0,1},{1,2},{2,3},{3,0},{4,5},{5,6},{6,7},{7,4},{8,9},{9,10},{10,1... | collective-permute-start | bytes 393224 | tf_op jit(solution)/shard_map/ppermute | solution.py:374
  8.9 8.5 %collective-permute-start.2 = (bf16[16,4096]{1,0:T(8,128)(2,1)S(1)}, bf16[16,4096]{1,0:T(8,128)(2,1)S(1)}, u32[]{:S(2)}, u32[]{:S(2)}) collective-permute-start(bf16[16,4096]{1,0:T(8,128)(2,1)S(1)} %get-tuple-element.19), channel_id=1, source_target_pairs={{0,2},{1,3},{2,0},{3,1},{4,6},{5,7},{6,4},{7,5},{8,10},{9,11},{10,... | collective-permute-start | bytes 393224 | tf_op jit(solution)/shard_map/ppermute | solution.py:374
  11.4 6.1 %collective-permute-start.3 = (bf16[16,4096]{1,0:T(8,128)(2,1)S(1)}, bf16[16,4096]{1,0:T(8,128)(2,1)S(1)}, u32[]{:S(2)}, u32[]{:S(2)}) collective-permute-start(bf16[16,4096]{1,0:T(8,128)(2,1)S(1)} %get-tuple-element.20), channel_id=1, source_target_pairs={{0,3},{1,0},{2,1},{3,2},{4,7},{5,4},{6,5},{7,6},{8,11},{9,8},{10,9... | collective-permute-start | bytes 393224 | tf_op jit(solution)/shard_map/ppermute | solution.py:374
  12.5 4.9 %copy-start = (bf16[16,4096]{1,0:T(8,128)(2,1)S(1)}, bf16[16,4096]{1,0:T(8,128)(2,1)}, u32[]{:S(2)}) copy-start(bf16[16,4096]{1,0:T(8,128)(2,1)} %refs_4_.1) | copy-start | bytes 393220
  12.5 4.9 %copy-start.1 = (s32[16,8]{0,1:T(8,128)S(1)}, s32[16,8]{0,1:T(8,128)}, u32[]{:S(2)}) copy-start(s32[16,8]{0,1:T(8,128)} %param.24) | copy-start | bytes 1540
  12.5 4.9 %copy-start.2 = (s32[16,8]{0,1:T(8,128)S(1)}, s32[16,8]{0,1:T(8,128)}, u32[]{:S(2)}) copy-start(s32[16,8]{0,1:T(8,128)} %param.25) | copy-start | bytes 1540
  12.5 4.9 %copy-start.3 = (f32[4096]{0:T(1024)S(1)}, f32[4096]{0:T(1024)}, u32[]{:S(2)}) copy-start(f32[4096]{0:T(1024)} %param.23) | copy-start | bytes 49156
  58.1 40.6 %copy-start.4 = (f32[16,8]{0,1:T(8,128)S(1)}, f32[16,8]{0,1:T(8,128)}, u32[]{:S(2)}) copy-start(f32[16,8]{0,1:T(8,128)} %param.26) | copy-start | bytes 1540

commit v4 on v3

--- a/solution.py
+++ b/solution.py
@@ -215,18 +215,20 @@
         copy.wait()
 
 
-def load(*weights):
+def load(weights, tables):
     size = sum(w.size * 2 for w in weights)
-    return pl.pallas_call(
+    arrays = [*weights, *tables]
+    out = pl.pallas_call(
         load_kernel,
-        in_specs=[whole(pltpu.HBM)] * len(weights),
-        out_specs=[whole()] * len(weights),
-        out_shape=[pltpu.VMEM(w.shape, w.dtype) for w in weights],
-        scratch_shapes=[pltpu.SemaphoreType.DMA((len(weights),))],
+        in_specs=[whole(pltpu.HBM)] * len(arrays),
+        out_specs=[whole()] * len(weights) + [whole(SMEM)] * len(tables),
+        out_shape=[pltpu.VMEM(w.shape, w.dtype) for w in weights] + [pltpu.SMEM(t.shape, t.dtype) for t in tables],
+        scratch_shapes=[pltpu.SemaphoreType.DMA((len(arrays),))],
         compiler_params=pltpu.CompilerParams(vmem_limit_bytes=2 * MIB),
         cost_estimate=pl.CostEstimate(flops=0, bytes_accessed=2 * size, transcendentals=0),
         name="load",
-    )(*[pltpu.with_memory_space_constraint(w, pltpu.HBM) for w in weights])
+    )(*[pltpu.with_memory_space_constraint(a, pltpu.HBM) for a in arrays])
+    return out[: len(weights)], out[len(weights) :]
 
 
 def expert_kernel(x_ref, wg_ref, wu_ref, wd_hbm, out_ref, wide_ref, flat_ref, hidden_ref, wd_ref, sem):
@@ -370,18 +372,18 @@
     )
     got = lax.ppermute(theirs, "sec", [(i, 1 - i) for i in range(sec_count)])
     quarters = quarter(kv, mine, got, group_count)
-    parts = [quarters[0]] + [
-        lax.ppermute(quarters[s], "kv", [(i, (i + s) % group_count) for i in range(group_count)])
-        for s in range(1, group_count)
-    ]
-    ids, slots, probs = expert_ids.T, expert_slots.T, gate_probs.T
+    parts = [quarters[0]]
+    for s in sorted(range(1, group_count), key=lambda s: min(s, group_count - s)):
+        parts.append(lax.ppermute(quarters[s], "kv", [(i, (i + s) % group_count) for i in range(group_count)]))
+    weights, tables = load((w_gate[0], w_up[0]), (expert_ids.T, expert_slots.T, gate_probs.T))
+    ids, slots, probs = tables
     stream, outgoing = route(ids, slots, parts, residual, norm_gain.reshape(1, width), expert_count, capacity)
 
     def exchange(rows):
         sent = rows.reshape(expert_count, capacity * pieces, LANES)
         return lax.all_to_all(sent, ("sec", "req", "kv"), split_axis=0, concat_axis=0, tiled=True)
 
-    outgoing, *weights = lax.optimization_barrier((outgoing, *load(w_gate[0], w_up[0])))
+    outgoing, *weights = lax.optimization_barrier((outgoing, *weights))
     arrived = exchange(outgoing).reshape(expert_count * capacity, pieces, LANES)
     finished = expert(arrived, *weights, w_down[0])
     returned = exchange(finished).reshape(expert_count, capacity, pieces, LANES)

time: 101 us -> 98.6 us (0.976)
  Pallas kernels: 17.9 us -> 16.6 us
where the time goes in v4:
time: 98.6 us; the launch traced here: 98.5 us
  blocking collectives  73 us (74%)
  Pallas kernels  16.6 us (17%)
  starting transfers between devices  5.86 us (6%)
  waiting for transfers between devices  2.31 us (2%)
    all_to_all x2, blocking collectives, exchange(): lax.all_to_all(sent, ('sec', 'req', 'kv'), split_axis=0, concat_axis=0, t...  73 us
    pallas_call x1, Pallas kernels, expert(): pl.pallas_call(expert_kernel, in_specs=[whole()] * 3 + [whole(pltpu.HBM)]...  6.15 us
    pallas_call x1, Pallas kernels, load(): pl.pallas_call(load_kernel, in_specs=[whole(pltpu.HBM)] * len(arrays), ou...  4.7 us
    ppermute x3, starting transfers between devices, on_device(): lax.ppermute(quarters[s], 'kv', [(i, (i + s) % group_count) for i in rang...  4.36 us
    pallas_call x1, Pallas kernels, attend(): pl.pallas_call(attend_kernel, in_specs=[whole(SMEM)] + [whole(pltpu.HBM)]...  3.74 us
  transfers between devices with their start and end apart: 4, of which 2 were waited for; matrix products, arithmetic and copies ran while one was open for 0% of the time, Pallas kernels for 5%

profile of v4, /device:TPU:1, one launch (start us, length us, event | category | flops | bytes accessed | tf_op | source)
XLA Modules:
  0.0 98.5 jit_solution(4986787318496774659)
XLA Ops:
  0.6 3.7 %attend.1 = (bf16[64,4096]{1,0:T(8,128)(2,1)S(1)}, bf16[64,4096]{1,0:T(8,128)(2,1)S(1)}) custom-call(s32[1]{0:T(128)} %bitcast.6.sec_ref, s32[1,128]{1,0:T(1,128)} %bitcast.33, bf16[128,512]{1,0:T(8,128)(2,1)} %q_hbm.1, bf16[4096,128]{1,0:T(8,128)(2,1)} %bitcast.26, bf16[4096,128]{1,0:T(8,128)(2,1)} %bitcast.27, bf16[128,128]{1,0:T(8,128)(2,1)} %bitcast.28, ...), custom_call_target="tpu_custom_call" | custom-call | tf_op jit(solution)/shard_map/attend/pallas_call | solution.py:119
  4.4 1.5 %collective-permute-start = (bf16[64,4096]{1,0:T(8,128)(2,1)S(1)}, bf16[64,4096]{1,0:T(8,128)(2,1)S(1)}, u32[]{:S(2)}, u32[]{:S(2)}) collective-permute-start(bf16[64,4096]{1,0:T(8,128)(2,1)S(1)} %get-tuple-element.21), channel_id=1, source_target_pairs={{0,64},{64,0},{1,65},{65,1},{2,66},{66,2},{3,67},{67,3},{4,68},{68... | collective-permute-start | bytes 1572872 | tf_op jit(solution)/shard_map/ppermute | solution.py:373
  5.9 1.5 %collective-permute-done.got_ref = bf16[64,4096]{1,0:T(8,128)(2,1)S(1)} collective-permute-done((bf16[64,4096]{1,0:T(8,128)(2,1)S(1)}, bf16[64,4096]{1,0:T(8,128)(2,1)S(1)}, u32[]{:S(2)}, u32[]{:S(2)}) %collective-permute-start) | collective-permute-done | bytes 524320 | tf_op jit(solution)/shard_map/ppermute | solution.py:373
  7.4 0.1 quarter.1
  7.6 1.4 %collective-permute-start.1 = (bf16[16,4096]{1,0:T(8,128)(2,1)S(1)}, bf16[16,4096]{1,0:T(8,128)(2,1)S(1)}, u32[]{:S(2)}, u32[]{:S(2)}) collective-permute-start(bf16[16,4096]{1,0:T(8,128)(2,1)S(1)} %get-tuple-element.23), channel_id=1, source_target_pairs={{0,1},{1,2},{2,3},{3,0},{4,5},{5,6},{6,7},{7,4},{8,9},{9,10},{10,1... | collective-permute-start | bytes 393224 | tf_op jit(solution)/shard_map/ppermute | solution.py:377
  8.9 1.4 %collective-permute-start.2 = (bf16[16,4096]{1,0:T(8,128)(2,1)S(1)}, bf16[16,4096]{1,0:T(8,128)(2,1)S(1)}, u32[]{:S(2)}, u32[]{:S(2)}) collective-permute-start(bf16[16,4096]{1,0:T(8,128)(2,1)S(1)} %get-tuple-element.24), channel_id=1, source_target_pairs={{0,3},{1,0},{2,1},{3,2},{4,7},{5,4},{6,5},{7,6},{8,11},{9,8},{10,9... | collective-permute-start | bytes 393224 | tf_op jit(solution)/shard_map/ppermute | solution.py:377
  10.3 1.6 %collective-permute-start.3 = (bf16[16,4096]{1,0:T(8,128)(2,1)S(1)}, bf16[16,4096]{1,0:T(8,128)(2,1)S(1)}, u32[]{:S(2)}, u32[]{:S(2)}) collective-permute-start(bf16[16,4096]{1,0:T(8,128)(2,1)S(1)} %get-tuple-element.25), channel_id=1, source_target_pairs={{0,2},{1,3},{2,0},{3,1},{4,6},{5,7},{6,4},{7,5},{8,10},{9,11},{10,... | collective-permute-start | bytes 393224 | tf_op jit(solution)/shard_map/ppermute | solution.py:377
  11.9 0.0 copy-start
  11.9 0.0 copy-start.1
  11.9 4.7 %load.1 = (bf16[4096,768]{1,0:T(8,128)(2,1)S(1)}, bf16[4096,768]{1,0:T(8,128)(2,1)S(1)}, s32[8,16]{1,0:T(8,128)S(4)}, s32[8,16]{1,0:T(8,128)S(4)}, f32[8,16]{1,0:T(8,128)S(4)}) custom-call(bf16[4096,768]{1,0:T(8,128)(2,1)} %bitcast.23, bf16[4096,768]{1,0:T(8,128)(2,1)} %bitcast.24, s32[8,16]{1,0:T(8,128)} %bitcast.30, s32[8,16]{1,0:T(8,128)} %bitcast.31, ...), custom_call_target="tpu_custom_call" | custom-call | bytes 25165824 | tf_op jit(solution)/shard_map/load/pallas_call | solution.py:221
  16.6 0.0 collective-permute-done.1.refs_1_
  16.6 0.0 collective-permute-done.2.refs_2_
  16.6 0.8 collective-permute-done.3.refs_3_
  17.4 0.0 copy-done
  17.4 0.0 copy-done.1
  17.4 0.8 route.1
  18.2 38.6 %all_to_all.10 = bf16[128,64,128]{2,1,0:T(8,128)(2,1)S(1)} all-to-all(bf16[128,64,128]{2,1,0:T(8,128)(2,1)S(1)} %bitcast.21), channel_id=1, replica_groups=mesh['sec'=2,'req'=16,'kv'=4] {'sec','req','kv'}, dimensions={0} | all-to-all | bytes 4194304 | tf_op jit(solution)/shard_map/all_to_all | solution.py:384
  56.8 6.1 %expert.1 = bf16[256,32,128]{2,1,0:T(8,128)(2,1)S(1)} custom-call(bf16[256,32,128]{2,1,0:T(8,128)(2,1)S(1)} %bitcast.19, bf16[4096,768]{1,0:T(8,128)(2,1)S(1)} %get-tuple-element.32.wg_ref, bf16[4096,768]{1,0:T(8,128)(2,1)S(1)} %get-tuple-element.33.wu_ref, bf16[768,4096]{1,0:T(8,128)(2,1)} %bitcast.25), custom_call_target="tpu_custom_call" | custom-call | tf_op jit(solution)/shard_map/expert/pallas_call | solution.py:285
  63.0 34.5 %all_to_all.11 = bf16[128,64,128]{2,1,0:T(8,128)(2,1)S(1)} all-to-all(bf16[128,64,128]{2,1,0:T(8,128)(2,1)S(1)} %bitcast.20), channel_id=1, replica_groups=mesh['sec'=2,'req'=16,'kv'=4] {'sec','req','kv'}, dimensions={0} | all-to-all | bytes 4194304 | tf_op jit(solution)/shard_map/all_to_all | solution.py:384
  97.4 1.1 %combine.1 = bf16[16,4096]{1,0:T(8,128)(2,1)} custom-call(s32[8,16]{1,0:T(8,128)S(4)} %get-tuple-element.18.ids_ref, s32[8,16]{1,0:T(8,128)S(4)} %get-tuple-element.19.slots_ref, f32[8,16]{1,0:T(8,128)S(4)} %get-tuple-element.27.probs_ref, bf16[128,2,32,128]{3,2,1,0:T(8,128)(2,1)S(1)} %bitcast.18), custom_call_target="tpu_custom_call" | custom-call | tf_op jit(solution)/shard_map/combine/pallas_call | solution.py:325
Async XLA Ops:
  4.4 3.0 %collective-permute-start = (bf16[64,4096]{1,0:T(8,128)(2,1)S(1)}, bf16[64,4096]{1,0:T(8,128)(2,1)S(1)}, u32[]{:S(2)}, u32[]{:S(2)}) collective-permute-start(bf16[64,4096]{1,0:T(8,128)(2,1)S(1)} %get-tuple-element.21), channel_id=1, source_target_pairs={{0,64},{64,0},{1,65},{65,1},{2,66},{66,2},{3,67},{67,3},{4,68},{68... | collective-permute-start | bytes 1572872 | tf_op jit(solution)/shard_map/ppermute | solution.py:373
  7.6 9.1 %collective-permute-start.1 = (bf16[16,4096]{1,0:T(8,128)(2,1)S(1)}, bf16[16,4096]{1,0:T(8,128)(2,1)S(1)}, u32[]{:S(2)}, u32[]{:S(2)}) collective-permute-start(bf16[16,4096]{1,0:T(8,128)(2,1)S(1)} %get-tuple-element.23), channel_id=1, source_target_pairs={{0,1},{1,2},{2,3},{3,0},{4,5},{5,6},{6,7},{7,4},{8,9},{9,10},{10,1... | collective-permute-start | bytes 393224 | tf_op jit(solution)/shard_map/ppermute | solution.py:377
  8.9 7.7 %collective-permute-start.2 = (bf16[16,4096]{1,0:T(8,128)(2,1)S(1)}, bf16[16,4096]{1,0:T(8,128)(2,1)S(1)}, u32[]{:S(2)}, u32[]{:S(2)}) collective-permute-start(bf16[16,4096]{1,0:T(8,128)(2,1)S(1)} %get-tuple-element.24), channel_id=1, source_target_pairs={{0,3},{1,0},{2,1},{3,2},{4,7},{5,4},{6,5},{7,6},{8,11},{9,8},{10,9... | collective-permute-start | bytes 393224 | tf_op jit(solution)/shard_map/ppermute | solution.py:377
  10.3 7.1 %collective-permute-start.3 = (bf16[16,4096]{1,0:T(8,128)(2,1)S(1)}, bf16[16,4096]{1,0:T(8,128)(2,1)S(1)}, u32[]{:S(2)}, u32[]{:S(2)}) collective-permute-start(bf16[16,4096]{1,0:T(8,128)(2,1)S(1)} %get-tuple-element.25), channel_id=1, source_target_pairs={{0,2},{1,3},{2,0},{3,1},{4,6},{5,7},{6,4},{7,5},{8,10},{9,11},{10,... | collective-permute-start | bytes 393224 | tf_op jit(solution)/shard_map/ppermute | solution.py:377
  11.9 5.5 %copy-start = (bf16[16,4096]{1,0:T(8,128)(2,1)S(1)}, bf16[16,4096]{1,0:T(8,128)(2,1)}, u32[]{:S(2)}) copy-start(bf16[16,4096]{1,0:T(8,128)(2,1)} %refs_4_.1) | copy-start | bytes 393220
  11.9 5.5 %copy-start.1 = (f32[4096]{0:T(1024)S(1)}, f32[4096]{0:T(1024)}, u32[]{:S(2)}) copy-start(f32[4096]{0:T(1024)} %param.23) | copy-start | bytes 49156

commit v5 on v4

--- a/solution.py
+++ b/solution.py
@@ -13,6 +13,7 @@
 MIB = 1 << 20
 
 GAP = 1
+SPARE = 40
 
 VMEM = pltpu.VMEM
 SMEM = pltpu.SMEM
@@ -196,7 +197,7 @@
             jax.ShapeDtypeStruct((expert_count, capacity, pieces, LANES), BF16),
         ],
         scratch_shapes=[
-            pltpu.VMEM((rows * (pieces + GAP), LANES), F32),
+            pltpu.VMEM((rows * (pieces + GAP) + SPARE, LANES), F32),
             pltpu.VMEM((rows, width), BF16),
             pltpu.SemaphoreType.DMA,
         ],
@@ -288,7 +289,7 @@
         out_specs=whole(),
         out_shape=jax.ShapeDtypeStruct(x.shape, BF16),
         scratch_shapes=[
-            pltpu.VMEM((rows * (pieces + GAP), LANES), F32),
+            pltpu.VMEM((rows * (pieces + GAP) + SPARE, LANES), F32),
             pltpu.VMEM((rows, width), BF16),
             pltpu.VMEM((rows, hidden_width), BF16),
             pltpu.VMEM(wd.shape, BF16),
@@ -327,7 +328,7 @@
         in_specs=[whole(SMEM)] * 3 + [whole()],
         out_specs=whole(),
         out_shape=jax.ShapeDtypeStruct((rows, width), BF16),
-        scratch_shapes=[pltpu.VMEM((rows * (width // LANES + GAP), LANES), F32)],
+        scratch_shapes=[pltpu.VMEM((rows * (width // LANES + GAP) + SPARE, LANES), F32)],
         compiler_params=pltpu.CompilerParams(vmem_limit_bytes=4 * MIB),
         name="combine",
     )(ids, slots, probs, returned)

time: 98.6 us -> 98.6 us (level)
  no operation moved by 1% of the time
where the time goes in v5:
time: 98.6 us; the launch traced here: 98.5 us
  blocking collectives  73 us (74%)
  Pallas kernels  16.6 us (17%)
  starting transfers between devices  5.86 us (6%)
  waiting for transfers between devices  2.31 us (2%)
    all_to_all x2, blocking collectives, exchange(): lax.all_to_all(sent, ('sec', 'req', 'kv'), split_axis=0, concat_axis=0, t...  73 us
    pallas_call x1, Pallas kernels, expert(): pl.pallas_call(expert_kernel, in_specs=[whole()] * 3 + [whole(pltpu.HBM)]...  6.15 us
    pallas_call x1, Pallas kernels, load(): pl.pallas_call(load_kernel, in_specs=[whole(pltpu.HBM)] * len(arrays), ou...  4.7 us
    ppermute x3, starting transfers between devices, on_device(): lax.ppermute(quarters[s], 'kv', [(i, (i + s) % group_count) for i in rang...  4.36 us
    pallas_call x1, Pallas kernels, attend(): pl.pallas_call(attend_kernel, in_specs=[whole(SMEM)] + [whole(pltpu.HBM)]...  3.74 us
  transfers between devices with their start and end apart: 4, of which 2 were waited for; matrix products, arithmetic and copies ran while one was open for 0% of the time, Pallas kernels for 5%

profile of v5, /device:TPU:1, one launch (start us, length us, event | category | flops | bytes accessed | tf_op | source)
XLA Modules:
  0.0 98.5 jit_solution(2946077086493541123)
XLA Ops:
  0.6 3.7 %attend.1 = (bf16[64,4096]{1,0:T(8,128)(2,1)S(1)}, bf16[64,4096]{1,0:T(8,128)(2,1)S(1)}) custom-call(s32[1]{0:T(128)} %bitcast.6.sec_ref, s32[1,128]{1,0:T(1,128)} %bitcast.33, bf16[128,512]{1,0:T(8,128)(2,1)} %q_hbm.1, bf16[4096,128]{1,0:T(8,128)(2,1)} %bitcast.26, bf16[4096,128]{1,0:T(8,128)(2,1)} %bitcast.27, bf16[128,128]{1,0:T(8,128)(2,1)} %bitcast.28, ...), custom_call_target="tpu_custom_call" | custom-call | tf_op jit(solution)/shard_map/attend/pallas_call | solution.py:120
  4.4 1.5 %collective-permute-start = (bf16[64,4096]{1,0:T(8,128)(2,1)S(1)}, bf16[64,4096]{1,0:T(8,128)(2,1)S(1)}, u32[]{:S(2)}, u32[]{:S(2)}) collective-permute-start(bf16[64,4096]{1,0:T(8,128)(2,1)S(1)} %get-tuple-element.21), channel_id=1, source_target_pairs={{0,64},{64,0},{1,65},{65,1},{2,66},{66,2},{3,67},{67,3},{4,68},{68... | collective-permute-start | bytes 1572872 | tf_op jit(solution)/shard_map/ppermute | solution.py:374
  5.9 1.5 %collective-permute-done.got_ref = bf16[64,4096]{1,0:T(8,128)(2,1)S(1)} collective-permute-done((bf16[64,4096]{1,0:T(8,128)(2,1)S(1)}, bf16[64,4096]{1,0:T(8,128)(2,1)S(1)}, u32[]{:S(2)}, u32[]{:S(2)}) %collective-permute-start) | collective-permute-done | bytes 524320 | tf_op jit(solution)/shard_map/ppermute | solution.py:374
  7.4 0.1 quarter.1
  7.6 1.4 %collective-permute-start.1 = (bf16[16,4096]{1,0:T(8,128)(2,1)S(1)}, bf16[16,4096]{1,0:T(8,128)(2,1)S(1)}, u32[]{:S(2)}, u32[]{:S(2)}) collective-permute-start(bf16[16,4096]{1,0:T(8,128)(2,1)S(1)} %get-tuple-element.23), channel_id=1, source_target_pairs={{0,1},{1,2},{2,3},{3,0},{4,5},{5,6},{6,7},{7,4},{8,9},{9,10},{10,1... | collective-permute-start | bytes 393224 | tf_op jit(solution)/shard_map/ppermute | solution.py:378
  8.9 1.4 %collective-permute-start.2 = (bf16[16,4096]{1,0:T(8,128)(2,1)S(1)}, bf16[16,4096]{1,0:T(8,128)(2,1)S(1)}, u32[]{:S(2)}, u32[]{:S(2)}) collective-permute-start(bf16[16,4096]{1,0:T(8,128)(2,1)S(1)} %get-tuple-element.24), channel_id=1, source_target_pairs={{0,3},{1,0},{2,1},{3,2},{4,7},{5,4},{6,5},{7,6},{8,11},{9,8},{10,9... | collective-permute-start | bytes 393224 | tf_op jit(solution)/shard_map/ppermute | solution.py:378
  10.3 1.6 %collective-permute-start.3 = (bf16[16,4096]{1,0:T(8,128)(2,1)S(1)}, bf16[16,4096]{1,0:T(8,128)(2,1)S(1)}, u32[]{:S(2)}, u32[]{:S(2)}) collective-permute-start(bf16[16,4096]{1,0:T(8,128)(2,1)S(1)} %get-tuple-element.25), channel_id=1, source_target_pairs={{0,2},{1,3},{2,0},{3,1},{4,6},{5,7},{6,4},{7,5},{8,10},{9,11},{10,... | collective-permute-start | bytes 393224 | tf_op jit(solution)/shard_map/ppermute | solution.py:378
  11.9 0.0 copy-start
  11.9 0.0 copy-start.1
  11.9 4.7 %load.1 = (bf16[4096,768]{1,0:T(8,128)(2,1)S(1)}, bf16[4096,768]{1,0:T(8,128)(2,1)S(1)}, s32[8,16]{1,0:T(8,128)S(4)}, s32[8,16]{1,0:T(8,128)S(4)}, f32[8,16]{1,0:T(8,128)S(4)}) custom-call(bf16[4096,768]{1,0:T(8,128)(2,1)} %bitcast.23, bf16[4096,768]{1,0:T(8,128)(2,1)} %bitcast.24, s32[8,16]{1,0:T(8,128)} %bitcast.30, s32[8,16]{1,0:T(8,128)} %bitcast.31, ...), custom_call_target="tpu_custom_call" | custom-call | bytes 25165824 | tf_op jit(solution)/shard_map/load/pallas_call | solution.py:222
  16.6 0.0 collective-permute-done.1.refs_1_
  16.6 0.0 collective-permute-done.2.refs_2_
  16.6 0.8 collective-permute-done.3.refs_3_
  17.4 0.0 copy-done
  17.4 0.0 copy-done.1
  17.4 0.8 route.1
  18.2 38.6 %all_to_all.10 = bf16[128,64,128]{2,1,0:T(8,128)(2,1)S(1)} all-to-all(bf16[128,64,128]{2,1,0:T(8,128)(2,1)S(1)} %bitcast.21), channel_id=1, replica_groups=mesh['sec'=2,'req'=16,'kv'=4] {'sec','req','kv'}, dimensions={0} | all-to-all | bytes 4194304 | tf_op jit(solution)/shard_map/all_to_all | solution.py:385
  56.8 6.2 %expert.1 = bf16[256,32,128]{2,1,0:T(8,128)(2,1)S(1)} custom-call(bf16[256,32,128]{2,1,0:T(8,128)(2,1)S(1)} %bitcast.19, bf16[4096,768]{1,0:T(8,128)(2,1)S(1)} %get-tuple-element.32.wg_ref, bf16[4096,768]{1,0:T(8,128)(2,1)S(1)} %get-tuple-element.33.wu_ref, bf16[768,4096]{1,0:T(8,128)(2,1)} %bitcast.25), custom_call_target="tpu_custom_call" | custom-call | tf_op jit(solution)/shard_map/expert/pallas_call | solution.py:286
  63.0 34.5 %all_to_all.11 = bf16[128,64,128]{2,1,0:T(8,128)(2,1)S(1)} all-to-all(bf16[128,64,128]{2,1,0:T(8,128)(2,1)S(1)} %bitcast.20), channel_id=1, replica_groups=mesh['sec'=2,'req'=16,'kv'=4] {'sec','req','kv'}, dimensions={0} | all-to-all | bytes 4194304 | tf_op jit(solution)/shard_map/all_to_all | solution.py:385
  97.4 1.1 %combine.1 = bf16[16,4096]{1,0:T(8,128)(2,1)} custom-call(s32[8,16]{1,0:T(8,128)S(4)} %get-tuple-element.18.ids_ref, s32[8,16]{1,0:T(8,128)S(4)} %get-tuple-element.19.slots_ref, f32[8,16]{1,0:T(8,128)S(4)} %get-tuple-element.27.probs_ref, bf16[128,2,32,128]{3,2,1,0:T(8,128)(2,1)S(1)} %bitcast.18), custom_call_target="tpu_custom_call" | custom-call | tf_op jit(solution)/shard_map/combine/pallas_call | solution.py:326
Async XLA Ops:
  4.4 3.0 %collective-permute-start = (bf16[64,4096]{1,0:T(8,128)(2,1)S(1)}, bf16[64,4096]{1,0:T(8,128)(2,1)S(1)}, u32[]{:S(2)}, u32[]{:S(2)}) collective-permute-start(bf16[64,4096]{1,0:T(8,128)(2,1)S(1)} %get-tuple-element.21), channel_id=1, source_target_pairs={{0,64},{64,0},{1,65},{65,1},{2,66},{66,2},{3,67},{67,3},{4,68},{68... | collective-permute-start | bytes 1572872 | tf_op jit(solution)/shard_map/ppermute | solution.py:374
  7.6 9.1 %collective-permute-start.1 = (bf16[16,4096]{1,0:T(8,128)(2,1)S(1)}, bf16[16,4096]{1,0:T(8,128)(2,1)S(1)}, u32[]{:S(2)}, u32[]{:S(2)}) collective-permute-start(bf16[16,4096]{1,0:T(8,128)(2,1)S(1)} %get-tuple-element.23), channel_id=1, source_target_pairs={{0,1},{1,2},{2,3},{3,0},{4,5},{5,6},{6,7},{7,4},{8,9},{9,10},{10,1... | collective-permute-start | bytes 393224 | tf_op jit(solution)/shard_map/ppermute | solution.py:378
  8.9 7.7 %collective-permute-start.2 = (bf16[16,4096]{1,0:T(8,128)(2,1)S(1)}, bf16[16,4096]{1,0:T(8,128)(2,1)S(1)}, u32[]{:S(2)}, u32[]{:S(2)}) collective-permute-start(bf16[16,4096]{1,0:T(8,128)(2,1)S(1)} %get-tuple-element.24), channel_id=1, source_target_pairs={{0,3},{1,0},{2,1},{3,2},{4,7},{5,4},{6,5},{7,6},{8,11},{9,8},{10,9... | collective-permute-start | bytes 393224 | tf_op jit(solution)/shard_map/ppermute | solution.py:378
  10.3 7.1 %collective-permute-start.3 = (bf16[16,4096]{1,0:T(8,128)(2,1)S(1)}, bf16[16,4096]{1,0:T(8,128)(2,1)S(1)}, u32[]{:S(2)}, u32[]{:S(2)}) collective-permute-start(bf16[16,4096]{1,0:T(8,128)(2,1)S(1)} %get-tuple-element.25), channel_id=1, source_target_pairs={{0,2},{1,3},{2,0},{3,1},{4,6},{5,7},{6,4},{7,5},{8,10},{9,11},{10,... | collective-permute-start | bytes 393224 | tf_op jit(solution)/shard_map/ppermute | solution.py:378
  11.9 5.5 %copy-start = (bf16[16,4096]{1,0:T(8,128)(2,1)S(1)}, bf16[16,4096]{1,0:T(8,128)(2,1)}, u32[]{:S(2)}) copy-start(bf16[16,4096]{1,0:T(8,128)(2,1)} %refs_4_.1) | copy-start | bytes 393220
  11.9 5.5 %copy-start.1 = (f32[4096]{0:T(1024)S(1)}, f32[4096]{0:T(1024)}, u32[]{:S(2)}) copy-start(f32[4096]{0:T(1024)} %param.23) | copy-start | bytes 49156

commit v6 on v5

--- a/solution.py
+++ b/solution.py
@@ -23,8 +23,12 @@
     return pl.BlockSpec(memory_space=space)
 
 
+BLOCKS = 4
+
+
 def attend_kernel(
     sec_ref,
+    kv_ref,
     len_hbm,
     q_hbm,
     kc_hbm,
@@ -50,6 +54,7 @@
     group = 8
     to_exponent = math.log2(math.e) / LANES**0.5
     half = rows // 2
+    far = half // BLOCKS
 
     small = [
         pltpu.make_async_copy(source, target, sems.at[i])
@@ -100,8 +105,11 @@
         out = jnp.dot(raised[g].astype(BF16), values, preferred_element_type=F32)
         outs.append((out + own_raised[g] * per_head(group_rows(nv_ref, g))) * inverse)
     for g in range(0, groups, 2):
-        place = lax.rem(g * group + half * (1 - sec_ref[0]), rows)
-        place = pl.multiple_of(place, 2 * group)
+        block, blocks = g * group // far, half // far
+        way = 1 - 2 * (block // blocks)
+        turned = lax.rem(way * (block % blocks - kv_ref[0]) + blocks + blocks // 2, blocks)
+        side = lax.rem(block // blocks + 1 - sec_ref[0], 2)
+        place = pl.multiple_of(side * half + turned * far, 2 * group)
         for h in range(heads):
             pair = [outs[g + j][h * group : (h + 1) * group] for j in range(2)]
             attn_ref[pl.ds(place, 2 * group), pl.ds(h * LANES, LANES)] = jnp.concatenate(pair, axis=0).astype(BF16)
@@ -112,16 +120,16 @@
     mine_ref[...] = proj[half:].astype(BF16)
 
 
-def attend(sec, lengths, q, kc, vc, nk, nv, wo):
+def attend(sec, kv, lengths, q, kc, vc, nk, nv, wo):
     rows, head_width = q.shape
     width = wo.shape[1]
-    out = jax.ShapeDtypeStruct((rows // 2, width), BF16)
+    out = [jax.ShapeDtypeStruct((rows // 2, width), BF16)]
     far = [pltpu.with_memory_space_constraint(a, pltpu.HBM) for a in (lengths, q, kc, vc, nk, nv, wo)]
     return pl.pallas_call(
         attend_kernel,
-        in_specs=[whole(SMEM)] + [whole(pltpu.HBM)] * 7,
-        out_specs=[whole(), whole()],
-        out_shape=[out, out],
+        in_specs=[whole(SMEM)] * 2 + [whole(pltpu.HBM)] * 7,
+        out_specs=[whole()] * 2,
+        out_shape=out * 2,
         scratch_shapes=[pltpu.VMEM(a.shape, a.dtype) for a in (lengths, q, kc, vc, nk, nv)]
         + [
             pltpu.VMEM(wo.shape, BF16),
@@ -130,28 +138,27 @@
         ],
         compiler_params=pltpu.CompilerParams(vmem_limit_bytes=14 * MIB),
         name="attend",
-    )(sec, *far)
-
-
-def quarter_kernel(kv_ref, mine_ref, got_ref, *out_refs):
-    count = len(out_refs)
-    rows = mine_ref.shape[0] // count
-    for step, out_ref in enumerate(out_refs):
-        at = pl.ds(pl.multiple_of(lax.rem(kv_ref[0] + step, count) * rows, rows), rows)
+    )(sec, kv, *far)
+
+
+def join_kernel(mine_ref, got_ref, *out_refs):
+    rows = out_refs[0].shape[0]
+    for i, out_ref in enumerate(out_refs):
+        at = pl.ds(i * rows, rows)
         out_ref[...] = (mine_ref[at, :].astype(F32) + got_ref[at, :].astype(F32)).astype(BF16)
 
 
-def quarter(kv, mine, got, count):
+def join(mine, got, parts):
     rows, width = mine.shape
-    out = jax.ShapeDtypeStruct((rows // count, width), BF16)
+    out = jax.ShapeDtypeStruct((rows // parts, width), BF16)
     return pl.pallas_call(
-        quarter_kernel,
-        in_specs=[whole(SMEM), whole(), whole()],
-        out_specs=[whole()] * count,
-        out_shape=[out] * count,
+        join_kernel,
+        in_specs=[whole(), whole()],
+        out_specs=[whole()] * parts,
+        out_shape=[out] * parts,
         compiler_params=pltpu.CompilerParams(vmem_limit_bytes=4 * MIB),
-        name="quarter",
-    )(kv, mine, got)
+        name="join",
+    )(mine, got)
 
 
 def route_kernel(ids_ref, slots_ref, *refs):
@@ -363,6 +370,7 @@
 
     theirs, mine = attend(
         sec,
+        kv,
         lengths.reshape(1, row_count),
         queries,
         key_cache.reshape(-1, LANES),
@@ -371,11 +379,20 @@
         new_values.reshape(row_count, LANES),
         out_proj,
     )
-    got = lax.ppermute(theirs, "sec", [(i, 1 - i) for i in range(sec_count)])
-    quarters = quarter(kv, mine, got, group_count)
-    parts = [quarters[0]]
-    for s in sorted(range(1, group_count), key=lambda s: min(s, group_count - s)):
-        parts.append(lax.ppermute(quarters[s], "kv", [(i, (i + s) % group_count) for i in range(group_count)]))
+
+    def other_core(x):
+        return lax.ppermute(x, "sec", [(i, 1 - i) for i in range(sec_count)])
+
+    def along(x, step):
+        pairs = [
+            (c * group_count + i, c * group_count + (i + step * (1 - 2 * c)) % group_count)
+            for c in range(sec_count)
+            for i in range(group_count)
+        ]
+        return lax.ppermute(x, ("sec", "kv"), pairs)
+
+    far, before, keep, after = join(mine, other_core(theirs), group_count)
+    parts = [keep, along(after, 1), along(before, -1), along(far, 2)]
     weights, tables = load((w_gate[0], w_up[0]), (expert_ids.T, expert_slots.T, gate_probs.T))
     ids, slots, probs = tables
     stream, outgoing = route(ids, slots, parts, residual, norm_gain.reshape(1, width), expert_count, capacity)

time: 98.6 us -> 98.6 us (level)
  blocking collectives: 73 us -> 71.9 us
  waiting for transfers between devices: 2.31 us -> 3.37 us
    all_to_all x2, blocking collectives: 73 us -> 71.9 us  [exchange(): lax.all_to_all(sent, ('sec', 'req', 'kv'), split_axis=0, concat_axis=0, t...]
    ppermute x4, waiting for transfers between devices: 2.31 us -> 3.37 us  [the longest x3 1.84 us: along(): return lax.ppermute(x, ('sec', 'kv'), pairs)]
where the time goes in v6:
time: 98.6 us; the launch traced here: 98.4 us
  blocking collectives  71.9 us (73%)
  Pallas kernels  16.6 us (17%)
  starting transfers between devices  5.86 us (6%)
  waiting for transfers between devices  3.37 us (3%)
    all_to_all x2, blocking collectives, exchange(): lax.all_to_all(sent, ('sec', 'req', 'kv'), split_axis=0, concat_axis=0, t...  71.9 us
    pallas_call x1, Pallas kernels, expert(): pl.pallas_call(expert_kernel, in_specs=[whole()] * 3 + [whole(pltpu.HBM)]...  6.15 us
    pallas_call x1, Pallas kernels, load(): pl.pallas_call(load_kernel, in_specs=[whole(pltpu.HBM)] * len(arrays), ou...  4.7 us
    ppermute x3, starting transfers between devices, along(): return lax.ppermute(x, ('sec', 'kv'), pairs)  4.36 us
    pallas_call x1, Pallas kernels, attend(): pl.pallas_call(attend_kernel, in_specs=[whole(SMEM)] * 2 + [whole(pltpu.H...  3.74 us
  transfers between devices with their start and end apart: 4, of which 2 were waited for; matrix products, arithmetic and copies ran while one was open for 0% of the time, Pallas kernels for 5%

profile of v6, /device:TPU:1, one launch (start us, length us, event | category | flops | bytes accessed | tf_op | source)
XLA Modules:
  0.0 98.4 jit_solution(9282862626868107321)
XLA Ops:
  0.6 3.7 %attend.1 = (bf16[64,4096]{1,0:T(8,128)(2,1)S(1)}, bf16[64,4096]{1,0:T(8,128)(2,1)S(1)}) custom-call(s32[1]{0:T(128)} %bitcast.5.sec_ref, s32[1]{0:T(128)} %bitcast.6.kv_ref, s32[1,128]{1,0:T(1,128)} %bitcast.33, bf16[128,512]{1,0:T(8,128)(2,1)} %q_hbm.1, bf16[4096,128]{1,0:T(8,128)(2,1)} %bitcast.26, bf16[4096,128]{1,0:T(8,128)(2,1)} %bitcast.27, ...), custom_call_target="tpu_custom_call" | custom-call | tf_op jit(solution)/shard_map/attend/pallas_call | solution.py:128
  4.4 1.5 %collective-permute-start = (bf16[64,4096]{1,0:T(8,128)(2,1)S(1)}, bf16[64,4096]{1,0:T(8,128)(2,1)S(1)}, u32[]{:S(2)}, u32[]{:S(2)}) collective-permute-start(bf16[64,4096]{1,0:T(8,128)(2,1)S(1)} %get-tuple-element.21), channel_id=1, source_target_pairs={{0,64},{64,0},{1,65},{65,1},{2,66},{66,2},{3,67},{67,3},{4,68},{68... | collective-permute-start | bytes 1572872 | tf_op jit(solution)/shard_map/ppermute | solution.py:384
  5.9 1.5 %collective-permute-done.got_ref = bf16[64,4096]{1,0:T(8,128)(2,1)S(1)} collective-permute-done((bf16[64,4096]{1,0:T(8,128)(2,1)S(1)}, bf16[64,4096]{1,0:T(8,128)(2,1)S(1)}, u32[]{:S(2)}, u32[]{:S(2)}) %collective-permute-start) | collective-permute-done | bytes 524320 | tf_op jit(solution)/shard_map/ppermute | solution.py:384
  7.4 0.1 join.1
  7.6 2.6 %collective-permute-start.1 = (bf16[16,4096]{1,0:T(8,128)(2,1)S(1)}, bf16[16,4096]{1,0:T(8,128)(2,1)S(1)}, u32[]{:S(2)}, u32[]{:S(2)}) collective-permute-start(bf16[16,4096]{1,0:T(8,128)(2,1)S(1)} %get-tuple-element.23), channel_id=1, source_target_pairs={{0,1},{1,2},{2,3},{3,0},{64,67},{65,64},{66,65},{67,66},{4,5},{5,6... | collective-permute-start | bytes 393224 | tf_op jit(solution)/shard_map/ppermute | solution.py:392
  10.2 0.0 collective-permute-start.2
  10.2 1.7 %collective-permute-start.3 = (bf16[16,4096]{1,0:T(8,128)(2,1)S(1)}, bf16[16,4096]{1,0:T(8,128)(2,1)S(1)}, u32[]{:S(2)}, u32[]{:S(2)}) collective-permute-start(bf16[16,4096]{1,0:T(8,128)(2,1)S(1)} %get-tuple-element.25), channel_id=1, source_target_pairs={{0,2},{1,3},{2,0},{3,1},{64,66},{65,67},{66,64},{67,65},{4,6},{5,7... | collective-permute-start | bytes 393224 | tf_op jit(solution)/shard_map/ppermute | solution.py:392
  11.9 0.0 copy-start
  11.9 0.0 copy-start.1
  11.9 4.7 %load.1 = (bf16[4096,768]{1,0:T(8,128)(2,1)S(1)}, bf16[4096,768]{1,0:T(8,128)(2,1)S(1)}, s32[8,16]{1,0:T(8,128)S(4)}, s32[8,16]{1,0:T(8,128)S(4)}, f32[8,16]{1,0:T(8,128)S(4)}) custom-call(bf16[4096,768]{1,0:T(8,128)(2,1)} %bitcast.23, bf16[4096,768]{1,0:T(8,128)(2,1)} %bitcast.24, s32[8,16]{1,0:T(8,128)} %bitcast.30, s32[8,16]{1,0:T(8,128)} %bitcast.31, ...), custom_call_target="tpu_custom_call" | custom-call | bytes 25165824 | tf_op jit(solution)/shard_map/load/pallas_call | solution.py:229
  16.6 0.0 collective-permute-done.1.refs_1_
  16.6 0.0 collective-permute-done.2.refs_2_
  16.6 1.8 %collective-permute-done.3.refs_3_ = bf16[16,4096]{1,0:T(8,128)(2,1)S(1)} collective-permute-done((bf16[16,4096]{1,0:T(8,128)(2,1)S(1)}, bf16[16,4096]{1,0:T(8,128)(2,1)S(1)}, u32[]{:S(2)}, u32[]{:S(2)}) %collective-permute-start.3) | collective-permute-done | bytes 131104 | tf_op jit(solution)/shard_map/ppermute | solution.py:392
  18.5 0.0 copy-done
  18.5 0.0 copy-done.1
  18.5 0.8 route.1
  19.3 37.5 %all_to_all.10 = bf16[128,64,128]{2,1,0:T(8,128)(2,1)S(1)} all-to-all(bf16[128,64,128]{2,1,0:T(8,128)(2,1)S(1)} %bitcast.21), channel_id=1, replica_groups=mesh['sec'=2,'req'=16,'kv'=4] {'sec','req','kv'}, dimensions={0} | all-to-all | bytes 4194304 | tf_op jit(solution)/shard_map/all_to_all | solution.py:402
  56.8 6.2 %expert.1 = bf16[256,32,128]{2,1,0:T(8,128)(2,1)S(1)} custom-call(bf16[256,32,128]{2,1,0:T(8,128)(2,1)S(1)} %bitcast.19, bf16[4096,768]{1,0:T(8,128)(2,1)S(1)} %get-tuple-element.32.wg_ref, bf16[4096,768]{1,0:T(8,128)(2,1)S(1)} %get-tuple-element.33.wu_ref, bf16[768,4096]{1,0:T(8,128)(2,1)} %bitcast.25), custom_call_target="tpu_custom_call" | custom-call | tf_op jit(solution)/shard_map/expert/pallas_call | solution.py:293
  62.9 34.5 %all_to_all.11 = bf16[128,64,128]{2,1,0:T(8,128)(2,1)S(1)} all-to-all(bf16[128,64,128]{2,1,0:T(8,128)(2,1)S(1)} %bitcast.20), channel_id=1, replica_groups=mesh['sec'=2,'req'=16,'kv'=4] {'sec','req','kv'}, dimensions={0} | all-to-all | bytes 4194304 | tf_op jit(solution)/shard_map/all_to_all | solution.py:402
  97.4 1.1 %combine.1 = bf16[16,4096]{1,0:T(8,128)(2,1)} custom-call(s32[8,16]{1,0:T(8,128)S(4)} %get-tuple-element.18.ids_ref, s32[8,16]{1,0:T(8,128)S(4)} %get-tuple-element.19.slots_ref, f32[8,16]{1,0:T(8,128)S(4)} %get-tuple-element.27.probs_ref, bf16[128,2,32,128]{3,2,1,0:T(8,128)(2,1)S(1)} %bitcast.18), custom_call_target="tpu_custom_call" | custom-call | tf_op jit(solution)/shard_map/combine/pallas_call | solution.py:333
Async XLA Ops:
  4.4 3.0 %collective-permute-start = (bf16[64,4096]{1,0:T(8,128)(2,1)S(1)}, bf16[64,4096]{1,0:T(8,128)(2,1)S(1)}, u32[]{:S(2)}, u32[]{:S(2)}) collective-permute-start(bf16[64,4096]{1,0:T(8,128)(2,1)S(1)} %get-tuple-element.21), channel_id=1, source_target_pairs={{0,64},{64,0},{1,65},{65,1},{2,66},{66,2},{3,67},{67,3},{4,68},{68... | collective-permute-start | bytes 1572872 | tf_op jit(solution)/shard_map/ppermute | solution.py:384
  7.6 9.1 %collective-permute-start.1 = (bf16[16,4096]{1,0:T(8,128)(2,1)S(1)}, bf16[16,4096]{1,0:T(8,128)(2,1)S(1)}, u32[]{:S(2)}, u32[]{:S(2)}) collective-permute-start(bf16[16,4096]{1,0:T(8,128)(2,1)S(1)} %get-tuple-element.23), channel_id=1, source_target_pairs={{0,1},{1,2},{2,3},{3,0},{64,67},{65,64},{66,65},{67,66},{4,5},{5,6... | collective-permute-start | bytes 393224 | tf_op jit(solution)/shard_map/ppermute | solution.py:392
  10.2 6.5 %collective-permute-start.2 = (bf16[16,4096]{1,0:T(8,128)(2,1)S(1)}, bf16[16,4096]{1,0:T(8,128)(2,1)S(1)}, u32[]{:S(2)}, u32[]{:S(2)}) collective-permute-start(bf16[16,4096]{1,0:T(8,128)(2,1)S(1)} %get-tuple-element.24), channel_id=1, source_target_pairs={{0,3},{1,0},{2,1},{3,2},{64,65},{65,66},{66,67},{67,64},{4,7},{5,4... | collective-permute-start | bytes 393224 | tf_op jit(solution)/shard_map/ppermute | solution.py:392
  10.2 8.3 %collective-permute-start.3 = (bf16[16,4096]{1,0:T(8,128)(2,1)S(1)}, bf16[16,4096]{1,0:T(8,128)(2,1)S(1)}, u32[]{:S(2)}, u32[]{:S(2)}) collective-permute-start(bf16[16,4096]{1,0:T(8,128)(2,1)S(1)} %get-tuple-element.25), channel_id=1, source_target_pairs={{0,2},{1,3},{2,0},{3,1},{64,66},{65,67},{66,64},{67,65},{4,6},{5,7... | collective-permute-start | bytes 393224 | tf_op jit(solution)/shard_map/ppermute | solution.py:392
  11.9 6.6 %copy-start = (bf16[16,4096]{1,0:T(8,128)(2,1)S(1)}, bf16[16,4096]{1,0:T(8,128)(2,1)}, u32[]{:S(2)}) copy-start(bf16[16,4096]{1,0:T(8,128)(2,1)} %refs_4_.1) | copy-start | bytes 393220
  11.9 6.6 %copy-start.1 = (f32[4096]{0:T(1024)S(1)}, f32[4096]{0:T(1024)}, u32[]{:S(2)}) copy-start(f32[4096]{0:T(1024)} %param.23) | copy-start | bytes 49156

commit v7 on v6

--- a/solution.py
+++ b/solution.py
@@ -276,11 +276,15 @@
                 wide_ref[pl.ds(r * stride + n * (dcols // LANES) + s, 8, stride=stride), :] = done[
                     r : r + 8, s * LANES : (s + 1) * LANES
                 ]
+        if (n + 1) * dcols * 2 == width:
+            for r in range(rows):
+                out_ref[r, : pieces // 2] = wide_ref[pl.ds(r * stride, pieces // 2), :].astype(BF16)
 
     def narrow(i, carry):
         base = pl.multiple_of(i * group, group)
         for r in range(group):
-            out_ref[base + r] = wide_ref[pl.ds((base + r) * stride, pieces), :].astype(BF16)
+            late = wide_ref[pl.ds((base + r) * stride + pieces // 2, pieces // 2), :]
+            out_ref[base + r, pieces // 2 :] = late.astype(BF16)
         return carry
 
     lax.fori_loop(0, rows // group, narrow, 0)
@@ -321,7 +325,7 @@
         wide_ref[pl.ds(t * stride, pieces), :] = total
         return carry
 
-    lax.fori_loop(0, rows, one, 0, unroll=4)
+    lax.fori_loop(0, rows, one, 0, unroll=True)
     for s in range(pieces):
         low = wide_ref[pl.ds(s, 8, stride=stride), :]
         high = wide_ref[pl.ds(8 * stride + s, 8, stride=stride), :]

time: 98.6 us -> 98.6 us (level)
  no operation moved by 1% of the time
where the time goes in v7:
time: 98.6 us; the launch traced here: 98.4 us
  blocking collectives  71.9 us (73%)
  Pallas kernels  16.6 us (17%)
  starting transfers between devices  5.86 us (6%)
  waiting for transfers between devices  3.37 us (3%)
    all_to_all x2, blocking collectives, exchange(): lax.all_to_all(sent, ('sec', 'req', 'kv'), split_axis=0, concat_axis=0, t...  71.9 us
    pallas_call x1, Pallas kernels, expert(): pl.pallas_call(expert_kernel, in_specs=[whole()] * 3 + [whole(pltpu.HBM)]...  6.2 us
    pallas_call x1, Pallas kernels, load(): pl.pallas_call(load_kernel, in_specs=[whole(pltpu.HBM)] * len(arrays), ou...  4.7 us
    ppermute x3, starting transfers between devices, along(): return lax.ppermute(x, ('sec', 'kv'), pairs)  4.36 us
    pallas_call x1, Pallas kernels, attend(): pl.pallas_call(attend_kernel, in_specs=[whole(SMEM)] * 2 + [whole(pltpu.H...  3.74 us
  transfers between devices with their start and end apart: 4, of which 2 were waited for; matrix products, arithmetic and copies ran while one was open for 0% of the time, Pallas kernels for 5%

profile of v7, /device:TPU:1, one launch (start us, length us, event | category | flops | bytes accessed | tf_op | source)
XLA Modules:
  0.0 98.4 jit_solution(1283834737260737079)
XLA Ops:
  0.6 3.7 %attend.1 = (bf16[64,4096]{1,0:T(8,128)(2,1)S(1)}, bf16[64,4096]{1,0:T(8,128)(2,1)S(1)}) custom-call(s32[1]{0:T(128)} %bitcast.5.sec_ref, s32[1]{0:T(128)} %bitcast.6.kv_ref, s32[1,128]{1,0:T(1,128)} %bitcast.33, bf16[128,512]{1,0:T(8,128)(2,1)} %q_hbm.1, bf16[4096,128]{1,0:T(8,128)(2,1)} %bitcast.26, bf16[4096,128]{1,0:T(8,128)(2,1)} %bitcast.27, ...), custom_call_target="tpu_custom_call" | custom-call | tf_op jit(solution)/shard_map/attend/pallas_call | solution.py:128
  4.4 1.5 %collective-permute-start = (bf16[64,4096]{1,0:T(8,128)(2,1)S(1)}, bf16[64,4096]{1,0:T(8,128)(2,1)S(1)}, u32[]{:S(2)}, u32[]{:S(2)}) collective-permute-start(bf16[64,4096]{1,0:T(8,128)(2,1)S(1)} %get-tuple-element.21), channel_id=1, source_target_pairs={{0,64},{64,0},{1,65},{65,1},{2,66},{66,2},{3,67},{67,3},{4,68},{68... | collective-permute-start | bytes 1572872 | tf_op jit(solution)/shard_map/ppermute | solution.py:388
  5.9 1.5 %collective-permute-done.got_ref = bf16[64,4096]{1,0:T(8,128)(2,1)S(1)} collective-permute-done((bf16[64,4096]{1,0:T(8,128)(2,1)S(1)}, bf16[64,4096]{1,0:T(8,128)(2,1)S(1)}, u32[]{:S(2)}, u32[]{:S(2)}) %collective-permute-start) | collective-permute-done | bytes 524320 | tf_op jit(solution)/shard_map/ppermute | solution.py:388
  7.4 0.1 join.1
  7.6 2.6 %collective-permute-start.1 = (bf16[16,4096]{1,0:T(8,128)(2,1)S(1)}, bf16[16,4096]{1,0:T(8,128)(2,1)S(1)}, u32[]{:S(2)}, u32[]{:S(2)}) collective-permute-start(bf16[16,4096]{1,0:T(8,128)(2,1)S(1)} %get-tuple-element.23), channel_id=1, source_target_pairs={{0,1},{1,2},{2,3},{3,0},{64,67},{65,64},{66,65},{67,66},{4,5},{5,6... | collective-permute-start | bytes 393224 | tf_op jit(solution)/shard_map/ppermute | solution.py:396
  10.2 0.0 collective-permute-start.2
  10.2 1.7 %collective-permute-start.3 = (bf16[16,4096]{1,0:T(8,128)(2,1)S(1)}, bf16[16,4096]{1,0:T(8,128)(2,1)S(1)}, u32[]{:S(2)}, u32[]{:S(2)}) collective-permute-start(bf16[16,4096]{1,0:T(8,128)(2,1)S(1)} %get-tuple-element.25), channel_id=1, source_target_pairs={{0,2},{1,3},{2,0},{3,1},{64,66},{65,67},{66,64},{67,65},{4,6},{5,7... | collective-permute-start | bytes 393224 | tf_op jit(solution)/shard_map/ppermute | solution.py:396
  11.9 0.0 copy-start
  11.9 0.0 copy-start.1
  11.9 4.7 %load.1 = (bf16[4096,768]{1,0:T(8,128)(2,1)S(1)}, bf16[4096,768]{1,0:T(8,128)(2,1)S(1)}, s32[8,16]{1,0:T(8,128)S(4)}, s32[8,16]{1,0:T(8,128)S(4)}, f32[8,16]{1,0:T(8,128)S(4)}) custom-call(bf16[4096,768]{1,0:T(8,128)(2,1)} %bitcast.23, bf16[4096,768]{1,0:T(8,128)(2,1)} %bitcast.24, s32[8,16]{1,0:T(8,128)} %bitcast.30, s32[8,16]{1,0:T(8,128)} %bitcast.31, ...), custom_call_target="tpu_custom_call" | custom-call | bytes 25165824 | tf_op jit(solution)/shard_map/load/pallas_call | solution.py:229
  16.6 0.0 collective-permute-done.1.refs_1_
  16.6 0.0 collective-permute-done.2.refs_2_
  16.6 1.8 %collective-permute-done.3.refs_3_ = bf16[16,4096]{1,0:T(8,128)(2,1)S(1)} collective-permute-done((bf16[16,4096]{1,0:T(8,128)(2,1)S(1)}, bf16[16,4096]{1,0:T(8,128)(2,1)S(1)}, u32[]{:S(2)}, u32[]{:S(2)}) %collective-permute-start.3) | collective-permute-done | bytes 131104 | tf_op jit(solution)/shard_map/ppermute | solution.py:396
  18.5 0.0 copy-done
  18.5 0.0 copy-done.1
  18.5 0.8 route.1
  19.3 37.5 %all_to_all.10 = bf16[128,64,128]{2,1,0:T(8,128)(2,1)S(1)} all-to-all(bf16[128,64,128]{2,1,0:T(8,128)(2,1)S(1)} %bitcast.21), channel_id=1, replica_groups=mesh['sec'=2,'req'=16,'kv'=4] {'sec','req','kv'}, dimensions={0} | all-to-all | bytes 4194304 | tf_op jit(solution)/shard_map/all_to_all | solution.py:406
  56.8 6.2 %expert.1 = bf16[256,32,128]{2,1,0:T(8,128)(2,1)S(1)} custom-call(bf16[256,32,128]{2,1,0:T(8,128)(2,1)S(1)} %bitcast.19, bf16[4096,768]{1,0:T(8,128)(2,1)S(1)} %get-tuple-element.32.wg_ref, bf16[4096,768]{1,0:T(8,128)(2,1)S(1)} %get-tuple-element.33.wu_ref, bf16[768,4096]{1,0:T(8,128)(2,1)} %bitcast.25), custom_call_target="tpu_custom_call" | custom-call | tf_op jit(solution)/shard_map/expert/pallas_call | solution.py:297
  63.0 34.5 %all_to_all.11 = bf16[128,64,128]{2,1,0:T(8,128)(2,1)S(1)} all-to-all(bf16[128,64,128]{2,1,0:T(8,128)(2,1)S(1)} %bitcast.20), channel_id=1, replica_groups=mesh['sec'=2,'req'=16,'kv'=4] {'sec','req','kv'}, dimensions={0} | all-to-all | bytes 4194304 | tf_op jit(solution)/shard_map/all_to_all | solution.py:406
  97.4 1.0 %combine.1 = bf16[16,4096]{1,0:T(8,128)(2,1)} custom-call(s32[8,16]{1,0:T(8,128)S(4)} %get-tuple-element.18.ids_ref, s32[8,16]{1,0:T(8,128)S(4)} %get-tuple-element.19.slots_ref, f32[8,16]{1,0:T(8,128)S(4)} %get-tuple-element.27.probs_ref, bf16[128,2,32,128]{3,2,1,0:T(8,128)(2,1)S(1)} %bitcast.18), custom_call_target="tpu_custom_call" | custom-call | tf_op jit(solution)/shard_map/combine/pallas_call | solution.py:337
Async XLA Ops:
  4.4 3.0 %collective-permute-start = (bf16[64,4096]{1,0:T(8,128)(2,1)S(1)}, bf16[64,4096]{1,0:T(8,128)(2,1)S(1)}, u32[]{:S(2)}, u32[]{:S(2)}) collective-permute-start(bf16[64,4096]{1,0:T(8,128)(2,1)S(1)} %get-tuple-element.21), channel_id=1, source_target_pairs={{0,64},{64,0},{1,65},{65,1},{2,66},{66,2},{3,67},{67,3},{4,68},{68... | collective-permute-start | bytes 1572872 | tf_op jit(solution)/shard_map/ppermute | solution.py:388
  7.6 9.1 %collective-permute-start.1 = (bf16[16,4096]{1,0:T(8,128)(2,1)S(1)}, bf16[16,4096]{1,0:T(8,128)(2,1)S(1)}, u32[]{:S(2)}, u32[]{:S(2)}) collective-permute-start(bf16[16,4096]{1,0:T(8,128)(2,1)S(1)} %get-tuple-element.23), channel_id=1, source_target_pairs={{0,1},{1,2},{2,3},{3,0},{64,67},{65,64},{66,65},{67,66},{4,5},{5,6... | collective-permute-start | bytes 393224 | tf_op jit(solution)/shard_map/ppermute | solution.py:396
  10.2 6.5 %collective-permute-start.2 = (bf16[16,4096]{1,0:T(8,128)(2,1)S(1)}, bf16[16,4096]{1,0:T(8,128)(2,1)S(1)}, u32[]{:S(2)}, u32[]{:S(2)}) collective-permute-start(bf16[16,4096]{1,0:T(8,128)(2,1)S(1)} %get-tuple-element.24), channel_id=1, source_target_pairs={{0,3},{1,0},{2,1},{3,2},{64,65},{65,66},{66,67},{67,64},{4,7},{5,4... | collective-permute-start | bytes 393224 | tf_op jit(solution)/shard_map/ppermute | solution.py:396
  10.2 8.3 %collective-permute-start.3 = (bf16[16,4096]{1,0:T(8,128)(2,1)S(1)}, bf16[16,4096]{1,0:T(8,128)(2,1)S(1)}, u32[]{:S(2)}, u32[]{:S(2)}) collective-permute-start(bf16[16,4096]{1,0:T(8,128)(2,1)S(1)} %get-tuple-element.25), channel_id=1, source_target_pairs={{0,2},{1,3},{2,0},{3,1},{64,66},{65,67},{66,64},{67,65},{4,6},{5,7... | collective-permute-start | bytes 393224 | tf_op jit(solution)/shard_map/ppermute | solution.py:396
  11.9 6.6 %copy-start = (bf16[16,4096]{1,0:T(8,128)(2,1)S(1)}, bf16[16,4096]{1,0:T(8,128)(2,1)}, u32[]{:S(2)}) copy-start(bf16[16,4096]{1,0:T(8,128)(2,1)} %refs_4_.1) | copy-start | bytes 393220
  11.9 6.6 %copy-start.1 = (f32[4096]{0:T(1024)S(1)}, f32[4096]{0:T(1024)}, u32[]{:S(2)}) copy-start(f32[4096]{0:T(1024)} %param.23) | copy-start | bytes 49156

commit v8 on v7

--- a/solution.py
+++ b/solution.py
@@ -266,7 +266,7 @@
         at = pl.ds(n * ncols, ncols)
         gate = jnp.dot(flat_ref[...], wg_ref[:, at], preferred_element_type=F32)
         up = jnp.dot(flat_ref[...], wu_ref[:, at], preferred_element_type=F32)
-        hidden_ref[:, at] = (gate / (1.0 + jnp.exp(-gate)) * up).astype(BF16)
+        hidden_ref[:, at] = (0.5 * gate * (1.0 + jnp.tanh(0.5 * gate)) * up).astype(BF16)
 
     down_copy.wait()
     for n in range(width // dcols):

time: 98.6 us -> 98.5 us (level)
  no operation moved by 1% of the time
where the time goes in v8:
time: 98.5 us; the launch traced here: 98.4 us
  blocking collectives  71.9 us (73%)
  Pallas kernels  16.5 us (17%)
  starting transfers between devices  5.86 us (6%)
  waiting for transfers between devices  3.37 us (3%)
    all_to_all x2, blocking collectives, exchange(): lax.all_to_all(sent, ('sec', 'req', 'kv'), split_axis=0, concat_axis=0, t...  71.9 us
    pallas_call x1, Pallas kernels, expert(): pl.pallas_call(expert_kernel, in_specs=[whole()] * 3 + [whole(pltpu.HBM)]...  6.17 us
    pallas_call x1, Pallas kernels, load(): pl.pallas_call(load_kernel, in_specs=[whole(pltpu.HBM)] * len(arrays), ou...  4.7 us
    ppermute x3, starting transfers between devices, along(): return lax.ppermute(x, ('sec', 'kv'), pairs)  4.36 us
    pallas_call x1, Pallas kernels, attend(): pl.pallas_call(attend_kernel, in_specs=[whole(SMEM)] * 2 + [whole(pltpu.H...  3.74 us
  transfers between devices with their start and end apart: 4, of which 2 were waited for; matrix products, arithmetic and copies ran while one was open for 0% of the time, Pallas kernels for 5%

profile of v8, /device:TPU:1, one launch (start us, length us, event | category | flops | bytes accessed | tf_op | source)
XLA Modules:
  0.0 98.4 jit_solution(9611131209361042322)
XLA Ops:
  0.6 3.7 %attend.1 = (bf16[64,4096]{1,0:T(8,128)(2,1)S(1)}, bf16[64,4096]{1,0:T(8,128)(2,1)S(1)}) custom-call(s32[1]{0:T(128)} %bitcast.5.sec_ref, s32[1]{0:T(128)} %bitcast.6.kv_ref, s32[1,128]{1,0:T(1,128)} %bitcast.33, bf16[128,512]{1,0:T(8,128)(2,1)} %q_hbm.1, bf16[4096,128]{1,0:T(8,128)(2,1)} %bitcast.26, bf16[4096,128]{1,0:T(8,128)(2,1)} %bitcast.27, ...), custom_call_target="tpu_custom_call" | custom-call | tf_op jit(solution)/shard_map/attend/pallas_call | solution.py:128
  4.4 1.5 %collective-permute-start = (bf16[64,4096]{1,0:T(8,128)(2,1)S(1)}, bf16[64,4096]{1,0:T(8,128)(2,1)S(1)}, u32[]{:S(2)}, u32[]{:S(2)}) collective-permute-start(bf16[64,4096]{1,0:T(8,128)(2,1)S(1)} %get-tuple-element.21), channel_id=1, source_target_pairs={{0,64},{64,0},{1,65},{65,1},{2,66},{66,2},{3,67},{67,3},{4,68},{68... | collective-permute-start | bytes 1572872 | tf_op jit(solution)/shard_map/ppermute | solution.py:388
  5.9 1.5 %collective-permute-done.got_ref = bf16[64,4096]{1,0:T(8,128)(2,1)S(1)} collective-permute-done((bf16[64,4096]{1,0:T(8,128)(2,1)S(1)}, bf16[64,4096]{1,0:T(8,128)(2,1)S(1)}, u32[]{:S(2)}, u32[]{:S(2)}) %collective-permute-start) | collective-permute-done | bytes 524320 | tf_op jit(solution)/shard_map/ppermute | solution.py:388
  7.4 0.1 join.1
  7.6 2.6 %collective-permute-start.1 = (bf16[16,4096]{1,0:T(8,128)(2,1)S(1)}, bf16[16,4096]{1,0:T(8,128)(2,1)S(1)}, u32[]{:S(2)}, u32[]{:S(2)}) collective-permute-start(bf16[16,4096]{1,0:T(8,128)(2,1)S(1)} %get-tuple-element.23), channel_id=1, source_target_pairs={{0,1},{1,2},{2,3},{3,0},{64,67},{65,64},{66,65},{67,66},{4,5},{5,6... | collective-permute-start | bytes 393224 | tf_op jit(solution)/shard_map/ppermute | solution.py:396
  10.2 0.0 collective-permute-start.2
  10.2 1.7 %collective-permute-start.3 = (bf16[16,4096]{1,0:T(8,128)(2,1)S(1)}, bf16[16,4096]{1,0:T(8,128)(2,1)S(1)}, u32[]{:S(2)}, u32[]{:S(2)}) collective-permute-start(bf16[16,4096]{1,0:T(8,128)(2,1)S(1)} %get-tuple-element.25), channel_id=1, source_target_pairs={{0,2},{1,3},{2,0},{3,1},{64,66},{65,67},{66,64},{67,65},{4,6},{5,7... | collective-permute-start | bytes 393224 | tf_op jit(solution)/shard_map/ppermute | solution.py:396
  11.9 0.0 copy-start
  11.9 0.0 copy-start.1
  11.9 4.7 %load.1 = (bf16[4096,768]{1,0:T(8,128)(2,1)S(1)}, bf16[4096,768]{1,0:T(8,128)(2,1)S(1)}, s32[8,16]{1,0:T(8,128)S(4)}, s32[8,16]{1,0:T(8,128)S(4)}, f32[8,16]{1,0:T(8,128)S(4)}) custom-call(bf16[4096,768]{1,0:T(8,128)(2,1)} %bitcast.23, bf16[4096,768]{1,0:T(8,128)(2,1)} %bitcast.24, s32[8,16]{1,0:T(8,128)} %bitcast.30, s32[8,16]{1,0:T(8,128)} %bitcast.31, ...), custom_call_target="tpu_custom_call" | custom-call | bytes 25165824 | tf_op jit(solution)/shard_map/load/pallas_call | solution.py:229
  16.6 0.0 collective-permute-done.1.refs_1_
  16.6 0.0 collective-permute-done.2.refs_2_
  16.6 1.8 %collective-permute-done.3.refs_3_ = bf16[16,4096]{1,0:T(8,128)(2,1)S(1)} collective-permute-done((bf16[16,4096]{1,0:T(8,128)(2,1)S(1)}, bf16[16,4096]{1,0:T(8,128)(2,1)S(1)}, u32[]{:S(2)}, u32[]{:S(2)}) %collective-permute-start.3) | collective-permute-done | bytes 131104 | tf_op jit(solution)/shard_map/ppermute | solution.py:396
  18.5 0.0 copy-done
  18.5 0.0 copy-done.1
  18.5 0.8 route.1
  19.3 37.5 %all_to_all.10 = bf16[128,64,128]{2,1,0:T(8,128)(2,1)S(1)} all-to-all(bf16[128,64,128]{2,1,0:T(8,128)(2,1)S(1)} %bitcast.21), channel_id=1, replica_groups=mesh['sec'=2,'req'=16,'kv'=4] {'sec','req','kv'}, dimensions={0} | all-to-all | bytes 4194304 | tf_op jit(solution)/shard_map/all_to_all | solution.py:406
  56.8 6.2 %expert.1 = bf16[256,32,128]{2,1,0:T(8,128)(2,1)S(1)} custom-call(bf16[256,32,128]{2,1,0:T(8,128)(2,1)S(1)} %bitcast.19, bf16[4096,768]{1,0:T(8,128)(2,1)S(1)} %get-tuple-element.32.wg_ref, bf16[4096,768]{1,0:T(8,128)(2,1)S(1)} %get-tuple-element.33.wu_ref, bf16[768,4096]{1,0:T(8,128)(2,1)} %bitcast.25), custom_call_target="tpu_custom_call" | custom-call | tf_op jit(solution)/shard_map/expert/pallas_call | solution.py:297
  62.9 34.5 %all_to_all.11 = bf16[128,64,128]{2,1,0:T(8,128)(2,1)S(1)} all-to-all(bf16[128,64,128]{2,1,0:T(8,128)(2,1)S(1)} %bitcast.20), channel_id=1, replica_groups=mesh['sec'=2,'req'=16,'kv'=4] {'sec','req','kv'}, dimensions={0} | all-to-all | bytes 4194304 | tf_op jit(solution)/shard_map/all_to_all | solution.py:406
  97.4 1.0 %combine.1 = bf16[16,4096]{1,0:T(8,128)(2,1)} custom-call(s32[8,16]{1,0:T(8,128)S(4)} %get-tuple-element.18.ids_ref, s32[8,16]{1,0:T(8,128)S(4)} %get-tuple-element.19.slots_ref, f32[8,16]{1,0:T(8,128)S(4)} %get-tuple-element.27.probs_ref, bf16[128,2,32,128]{3,2,1,0:T(8,128)(2,1)S(1)} %bitcast.18), custom_call_target="tpu_custom_call" | custom-call | tf_op jit(solution)/shard_map/combine/pallas_call | solution.py:337
Async XLA Ops:
  4.4 3.0 %collective-permute-start = (bf16[64,4096]{1,0:T(8,128)(2,1)S(1)}, bf16[64,4096]{1,0:T(8,128)(2,1)S(1)}, u32[]{:S(2)}, u32[]{:S(2)}) collective-permute-start(bf16[64,4096]{1,0:T(8,128)(2,1)S(1)} %get-tuple-element.21), channel_id=1, source_target_pairs={{0,64},{64,0},{1,65},{65,1},{2,66},{66,2},{3,67},{67,3},{4,68},{68... | collective-permute-start | bytes 1572872 | tf_op jit(solution)/shard_map/ppermute | solution.py:388
  7.6 9.1 %collective-permute-start.1 = (bf16[16,4096]{1,0:T(8,128)(2,1)S(1)}, bf16[16,4096]{1,0:T(8,128)(2,1)S(1)}, u32[]{:S(2)}, u32[]{:S(2)}) collective-permute-start(bf16[16,4096]{1,0:T(8,128)(2,1)S(1)} %get-tuple-element.23), channel_id=1, source_target_pairs={{0,1},{1,2},{2,3},{3,0},{64,67},{65,64},{66,65},{67,66},{4,5},{5,6... | collective-permute-start | bytes 393224 | tf_op jit(solution)/shard_map/ppermute | solution.py:396
  10.2 6.5 %collective-permute-start.2 = (bf16[16,4096]{1,0:T(8,128)(2,1)S(1)}, bf16[16,4096]{1,0:T(8,128)(2,1)S(1)}, u32[]{:S(2)}, u32[]{:S(2)}) collective-permute-start(bf16[16,4096]{1,0:T(8,128)(2,1)S(1)} %get-tuple-element.24), channel_id=1, source_target_pairs={{0,3},{1,0},{2,1},{3,2},{64,65},{65,66},{66,67},{67,64},{4,7},{5,4... | collective-permute-start | bytes 393224 | tf_op jit(solution)/shard_map/ppermute | solution.py:396
  10.2 8.3 %collective-permute-start.3 = (bf16[16,4096]{1,0:T(8,128)(2,1)S(1)}, bf16[16,4096]{1,0:T(8,128)(2,1)S(1)}, u32[]{:S(2)}, u32[]{:S(2)}) collective-permute-start(bf16[16,4096]{1,0:T(8,128)(2,1)S(1)} %get-tuple-element.25), channel_id=1, source_target_pairs={{0,2},{1,3},{2,0},{3,1},{64,66},{65,67},{66,64},{67,65},{4,6},{5,7... | collective-permute-start | bytes 393224 | tf_op jit(solution)/shard_map/ppermute | solution.py:396
  11.9 6.6 %copy-start = (bf16[16,4096]{1,0:T(8,128)(2,1)S(1)}, bf16[16,4096]{1,0:T(8,128)(2,1)}, u32[]{:S(2)}) copy-start(bf16[16,4096]{1,0:T(8,128)(2,1)} %refs_4_.1) | copy-start | bytes 393220
  11.9 6.6 %copy-start.1 = (f32[4096]{0:T(1024)S(1)}, f32[4096]{0:T(1024)}, u32[]{:S(2)}) copy-start(f32[4096]{0:T(1024)} %param.23) | copy-start | bytes 49156
